TPU v7x, 32 devices: a whole 2x2x4 slice. The times are simulated.
32 devices in a mesh: pos: 16 (over z, y, x), mode: 2 (over core).
Axes of the slice: x: 2, y: 2, z: 4, core: 2. Of those that a mesh axis runs over, the one named last changes fastest.
Arguments:
- object_field: float32 [2, 2048, 512], P(None, 'pos'), may hold values from -6 to 6
- probe: float32 [2, 8, 256, 256], P(None, 'mode'), may hold values from -3 to 3
- measured: float32 [48, 256, 256], P('pos'), may hold values from 0 to 16
- row_offsets: int32 [48], P('pos'), may hold values from 0 to 127
- col_offsets: int32 [48], P('pos'), may hold values from 0 to 256
- tile_counts: int32 [16], P('pos'), may hold values from 1 to 3, 24 in all
Outputs:
- updated_object: float32 [2, 2048, 512], P(None, ('pos', 'mode'))
Inputs may be any that keep to these rules, and one draw needn't show every extreme that they name: Slots 0 to tile_counts[t] - 1 of tile t hold scan positions, the others are empty; the counts sum to 24 and the largest equals 3.
All inputs are finite; a program needn't handle non-finite values. No bound on the sum of `tile_counts` on one device may be relied on, other than what follows from the above.
Results may differ from a plain program's by a relative error of at most 0.0016.
Values sent between devices are 32-bit elements; how exact they have to be, the bound alone decides.
A program may use at most 64 MiB of HBM per device.

v0:
```python
import math

import jax
import jax.numpy as jnp
from jax import lax
from jax.sharding import PartitionSpec as P


def extended_2(array, sides, width):
    for axis, dim in sides:
        size, length = (lax.axis_size(axis), array.shape[dim])
        up = [(i, (i + 1) % size) for i in range(size - 1)]
        down = [(j, i) for i, j in up]
        last = lax.slice_in_dim(array, length - width, length, axis=dim)
        first = lax.slice_in_dim(array, 0, width, axis=dim)
        before = lax.ppermute(last, axis, up)
        after = lax.ppermute(first, axis, down)
        array = jnp.concatenate([before, array, after], axis=dim)
    return array


def dft_tables(pattern):
    counter = jnp.arange(pattern, dtype=jnp.int32)
    phases = counter[:, None] * counter[None, :] % pattern
    angles = phases.astype(jnp.float32) * (2.0 * math.pi / pattern)
    factor = 1.0 / math.sqrt(pattern)
    return (
        (jnp.cos(angles) * factor).astype(jnp.bfloat16),
        (-jnp.sin(angles) * factor).astype(jnp.bfloat16),
    )


def left_product(table, stacked):
    return jnp.einsum("ua,kab->kub", table, stacked, preferred_element_type=jnp.float32)


def right_product(stacked, table):
    return jnp.einsum("kub,bv->kuv", stacked, table, preferred_element_type=jnp.float32)


def local(object_field, probe, measured, row_offsets, col_offsets, tile_counts):
    rows_tile = object_field.shape[1]
    columns = object_field.shape[2]
    pattern = probe.shape[2]
    slot_count = measured.shape[0]
    mode_count = lax.axis_size("mode")
    my_mode = lax.axis_index("mode")
    share_rows = rows_tile // mode_count
    real_table, imag_table = dft_tables(pattern)
    anchor = jnp.zeros((), jnp.int32)
    extended = extended_2(object_field, (("pos", 1),), rows_tile)
    probe_re = probe[0]
    probe_im = probe[1]
    top_rows = rows_tile + row_offsets - pattern // 2

    def forward(position):
        window = lax.dynamic_slice(
            extended, (anchor, top_rows[position], col_offsets[position]), (2, pattern, pattern)
        )
        exit_re = (probe_re * window[0] - probe_im * window[1]).astype(jnp.bfloat16)
        exit_im = (probe_re * window[1] + probe_im * window[0]).astype(jnp.bfloat16)
        half_re = (left_product(real_table, exit_re) - left_product(imag_table, exit_im)).astype(
            jnp.bfloat16
        )
        half_im = (left_product(real_table, exit_im) + left_product(imag_table, exit_re)).astype(
            jnp.bfloat16
        )
        wave_re = right_product(half_re, real_table) - right_product(half_im, imag_table)
        wave_im = right_product(half_re, imag_table) + right_product(half_im, real_table)
        return (exit_re, exit_im, wave_re, wave_im)

    exit_re, exit_im, wave_re, wave_im = lax.map(forward, jnp.arange(slot_count, dtype=jnp.int32))
    power_sum = jnp.sum(wave_re * wave_re + wave_im * wave_im, axis=1)
    model_power = lax.psum(power_sum, "mode")
    scaling = jnp.sqrt(measured) / jnp.maximum(jnp.sqrt(model_power), 1.0)
    probe_power = jnp.sum(probe_re * probe_re + probe_im * probe_im, axis=0)
    live_count = tile_counts[0]

    def backward(position, buffer):
        fixed_re = (scaling[position] * wave_re[position]).astype(jnp.bfloat16)
        fixed_im = (scaling[position] * wave_im[position]).astype(jnp.bfloat16)
        back_re = (left_product(real_table, fixed_re) + left_product(imag_table, fixed_im)).astype(
            jnp.bfloat16
        )
        back_im = (left_product(real_table, fixed_im) - left_product(imag_table, fixed_re)).astype(
            jnp.bfloat16
        )
        delta_re = (
            right_product(back_re, real_table)
            + right_product(back_im, imag_table)
            - exit_re[position].astype(jnp.float32)
        )
        delta_im = (
            right_product(back_im, real_table)
            - right_product(back_re, imag_table)
            - exit_im[position].astype(jnp.float32)
        )
        numer_re = jnp.sum(probe_re * delta_re + probe_im * delta_im, axis=0)
        numer_im = jnp.sum(probe_re * delta_im - probe_im * delta_re, axis=0)
        contrib = jnp.stack([numer_re, numer_im, probe_power])
        contrib = jnp.where(position < live_count, contrib, jnp.zeros_like(contrib))
        corner = (anchor, top_rows[position], col_offsets[position])
        current = lax.dynamic_slice(buffer, corner, (3, pattern, pattern))
        return lax.dynamic_update_slice(buffer, current + contrib, corner)

    buffer = lax.fori_loop(
        0, slot_count, backward, jnp.zeros((3, 3 * rows_tile, columns), jnp.float32)
    )
    blocked = buffer.reshape(3, 3, rows_tile, columns)
    shared = lax.psum_scatter(blocked, "mode", scatter_dimension=2, tiled=True)
    outside = jnp.concatenate([shared[:, 0], shared[:, 2]], axis=1)
    framed_sum = extended_2(outside, (("pos", 1),), share_rows)
    update_sum = shared[:, 1] + framed_sum[:, :share_rows] + framed_sum[:, 3 * share_rows :]
    own_rows = lax.dynamic_slice_in_dim(object_field, my_mode * share_rows, share_rows, 1)
    return own_rows + update_sum[:2] / (update_sum[2] + 1.0)


def solution(mesh):
    in_specs = (
        P(None, "pos", None),
        P(None, "mode", None, None),
        P("pos", None, None),
        P("pos"),
        P("pos"),
        P("pos"),
    )
    out_specs = P(None, ("pos", "mode"), None)
    return jax.shard_map(local, mesh=mesh, in_specs=in_specs, out_specs=out_specs, check_vma=False)
```

profile of v0, /device:TPU:0, one launch (start us, length us, event | category | flops | bytes accessed | tf_op | source)
XLA Modules:
  0.0 298.3 jit_solution(1173094023289202451)
XLA Ops:
  7.8 4.9 %collective-permute-start = (f32[2,128,512]{1,2,0:T(8,128)S(1)}, f32[2,128,512]{1,2,0:T(8,128)S(1)}, u32[]{:S(2)}, u32[]{:S(2)}) collective-permute-start(f32[2,128,512]{1,2,0:T(8,128)S(1)} %copy.53), channel_id=1, source_target_pairs={{0,2},{2,4},{4,6},{6,8},{8,10},{10,12},{12,14},{14,16},{16,18},{18... | collective-permute-start | bytes 1572872 | tf_op jit(solution)/shard_map/ppermute | solution.py:16
  14.0 2.7 slice_bitcast_fusion
  19.3 15.7 %collective-permute-done = f32[2,128,512]{1,2,0:T(8,128)S(1)} collective-permute-done((f32[2,128,512]{1,2,0:T(8,128)S(1)}, f32[2,128,512]{1,2,0:T(8,128)S(1)}, u32[]{:S(2)}, u32[]{:S(2)}) %collective-permute-start) | collective-permute-done | bytes 524320 | tf_op jit(solution)/shard_map/ppermute | solution.py:16
  37.1 2.3 pad_maximum_fusion
  39.4 67.5 %while.33 = (s32[]{:T(128)}, bf16[3,4,256,256]{2,3,1,0:T(8,128)(2,1)}, bf16[3,4,256,256]{2,3,1,0:T(8,128)(2,1)}, f32[3,4,256,256]{3,2,1,0:T(8,128)}, f32[3,4,256...) while((s32[]{:T(128)}, ...), condition=%wide.region_1.2_spmd.clone.clone, body=%wide.region_0.1_spmd.clone.clone.sunk | while | flops 1088159744 | bytes 24119104 | solution.py:72
  54.9 2.2 fusion.243
  58.4 2.2 fusion.241
  80.9 2.3 fusion.241
  99.9 2.3 fusion.243
  103.4 2.3 fusion.241
  106.9 4.5 %add_reduce_fusion.1 = f32[3,256,256]{2,1,0:T(8,128)} fusion(f32[3,4,256,256]{3,2,1,0:T(8,128)} %get-tuple-element.856, f32[3,4,256,256]{3,2,1,0:T(8,128)} %get-tuple-element.855), kind=kLoop, calls=%fused_computation.167 | loop fusion | flops 2949120 | bytes 7077888 | tf_op jit(solution)/shard_map/reduce_sum | solution.py:73
  112.4 18.8 %all-reduce.2.cloned.1.call-done = f32[3,256,256]{2,1,0:T(8,128)} async-done(((f32[3,256,256]{2,1,0:T(8,128)}), f32[3,256,256]{2,1,0:T(8,128)}) %all-reduce.2.cloned.1.call-update) | async-done | bytes 786448 | tf_op jit(solution)/shard_map/psum | solution.py:74
  131.2 2.5 maximum_divide_fusion
  135.4 118.8 %while.34 = (s32[]{:T(128)}, f32[3,384,512]{2,1,0:T(8,128)}, s32[3]{0:T(128)S(1)}, s32[3]{0:T(128)S(1)}, s32[]{:T(128)}, /*index=5*/f32[3,256,256]{2,1,0:T(8,128...) while((s32[]{:T(128)}, f32[3,384,512]{2,1,0:T(8,128)}, ...), condition=%wide.region_8.9_spmd.clone.clone, body=%wide.region_5.8_spmd.clone.clone.sunk | while | flops 1089863680 | bytes 43254092 | solution.py:106
  138.6 2.2 fusion.262
  141.2 3.3 %fusion.263 = bf16[4,256,256]{1,2,0:T(8,128)(2,1)} fusion(f32[4,256,256]{2,1,0:T(8,128)} %fusion.262, f32[1,4,256,256]{2,3,1,0:T(8,128)S(1)} %copy.85, f32[256,256]{0,1:T(8,128)S(1)} %bitcast.240), kind=kOutput, calls=%fused_computation.95.clone.1 | convolution fusion | flops 136380416 | bytes 2883584 | tf_op jit(solution)/shard_map/while/body/eval_jaxpr/ua,kab->kub/dot_general | solution.py:34
  147.0 2.2 fusion.261
  150.8 2.5 fusion.264
  155.7 3.5 %add_reduce_fusion.4 = (f32[256,256]{1,0:T(8,128)S(1)}, f32[256,256]{1,0:T(8,128)S(1)}) fusion(f32[4,256,256]{2,1,0:T(8,128)} %get-tuple-element.894, f32[4,256,256]{2,1,0:T(8,128)} %get-tuple-element.892, f32[4,256,256]{2,1,0:T(8,128)S(1)} %fusion.264, bf16[1,4,256,256]{3,2,1,0:T(8,128)(2,1)S(1)} %copy.89, f32[4,256,256]{2,1,0:T(8,128)} %fusion.265, ...), kind=kOutput, calls=%fused_computation.102.clone.1 | convolution fusion | flops 138084352 | bytes 5767168 | tf_op jit(solution)/shard_map/while/body/eval_jaxpr/kub,bv->kuv/dot_general | solution.py:38
  166.0 9.3 %dynamic_update_slice.42 = f32[3,384,512]{2,1,0:T(8,128)} dynamic-update-slice(f32[3,384,512]{2,1,0:T(8,128)} %get-tuple-element.867, f32[3,256,256]{2,1,0:T(8,128)S(1)} %fusion.266, s32[]{:T(128)} %constant.88.clone.1..sunk.1, s32[]{:T(128)S(6)} %select_n.210, s32[]{:T(128)S(6)} %select_n.211) | dynamic-update-slice | bytes 1572868 | tf_op jit(solution)/shard_map/while/body/eval_jaxpr/dynamic_update_slice | solution.py:104
  178.5 2.3 fusion.262
  181.1 3.3 %fusion.263 = bf16[4,256,256]{1,2,0:T(8,128)(2,1)} fusion(f32[4,256,256]{2,1,0:T(8,128)} %fusion.262, f32[1,4,256,256]{2,3,1,0:T(8,128)S(1)} %copy.85, f32[256,256]{0,1:T(8,128)S(1)} %bitcast.240), kind=kOutput, calls=%fused_computation.95.clone.1 | convolution fusion | flops 136380416 | bytes 2883584 | tf_op jit(solution)/shard_map/while/body/eval_jaxpr/ua,kab->kub/dot_general | solution.py:34
  190.7 2.5 fusion.264
  195.6 3.5 %add_reduce_fusion.4 = (f32[256,256]{1,0:T(8,128)S(1)}, f32[256,256]{1,0:T(8,128)S(1)}) fusion(f32[4,256,256]{2,1,0:T(8,128)} %get-tuple-element.894, f32[4,256,256]{2,1,0:T(8,128)} %get-tuple-element.892, f32[4,256,256]{2,1,0:T(8,128)S(1)} %fusion.264, bf16[1,4,256,256]{3,2,1,0:T(8,128)(2,1)S(1)} %copy.89, f32[4,256,256]{2,1,0:T(8,128)} %fusion.265, ...), kind=kOutput, calls=%fused_computation.102.clone.1 | convolution fusion | flops 138084352 | bytes 5767168 | tf_op jit(solution)/shard_map/while/body/eval_jaxpr/kub,bv->kuv/dot_general | solution.py:38
  205.9 8.9 %dynamic_update_slice.42 = f32[3,384,512]{2,1,0:T(8,128)} dynamic-update-slice(f32[3,384,512]{2,1,0:T(8,128)} %get-tuple-element.867, f32[3,256,256]{2,1,0:T(8,128)S(1)} %fusion.266, s32[]{:T(128)} %constant.88.clone.1..sunk.1, s32[]{:T(128)S(6)} %select_n.210, s32[]{:T(128)S(6)} %select_n.211) | dynamic-update-slice | bytes 1572868 | tf_op jit(solution)/shard_map/while/body/eval_jaxpr/dynamic_update_slice | solution.py:104
  220.6 3.3 %fusion.263 = bf16[4,256,256]{1,2,0:T(8,128)(2,1)} fusion(f32[4,256,256]{2,1,0:T(8,128)} %fusion.262, f32[1,4,256,256]{2,3,1,0:T(8,128)S(1)} %copy.85, f32[256,256]{0,1:T(8,128)S(1)} %bitcast.240), kind=kOutput, calls=%fused_computation.95.clone.1 | convolution fusion | flops 136380416 | bytes 2883584 | tf_op jit(solution)/shard_map/while/body/eval_jaxpr/ua,kab->kub/dot_general | solution.py:34
  230.2 2.5 fusion.264
  235.1 3.5 %add_reduce_fusion.4 = (f32[256,256]{1,0:T(8,128)S(1)}, f32[256,256]{1,0:T(8,128)S(1)}) fusion(f32[4,256,256]{2,1,0:T(8,128)} %get-tuple-element.894, f32[4,256,256]{2,1,0:T(8,128)} %get-tuple-element.892, f32[4,256,256]{2,1,0:T(8,128)S(1)} %fusion.264, bf16[1,4,256,256]{3,2,1,0:T(8,128)(2,1)S(1)} %copy.89, f32[4,256,256]{2,1,0:T(8,128)} %fusion.265, ...), kind=kOutput, calls=%fused_computation.102.clone.1 | convolution fusion | flops 138084352 | bytes 5767168 | tf_op jit(solution)/shard_map/while/body/eval_jaxpr/kub,bv->kuv/dot_general | solution.py:38
  245.4 8.8 %dynamic_update_slice.42 = f32[3,384,512]{2,1,0:T(8,128)} dynamic-update-slice(f32[3,384,512]{2,1,0:T(8,128)} %get-tuple-element.867, f32[3,256,256]{2,1,0:T(8,128)S(1)} %fusion.266, s32[]{:T(128)} %constant.88.clone.1..sunk.1, s32[]{:T(128)S(6)} %select_n.210, s32[]{:T(128)S(6)} %select_n.211) | dynamic-update-slice | bytes 1572868 | tf_op jit(solution)/shard_map/while/body/eval_jaxpr/dynamic_update_slice | solution.py:104
  254.2 11.3 %reduce-scatter.2.cloned.1.call-done = f32[3,3,64,512]{3,2,1,0:T(8,128)} async-done(((f32[3,3,128,512]{3,2,1,0:T(8,128)}), f32[3,3,64,512]{3,2,1,0:T(8,128)}) %reduce-scatter.2.cloned.1.call-update) | async-done | bytes 1179664 | tf_op jit(solution)/shard_map/reduce_scatter | solution.py:110
  266.7 3.6 %collective-permute-start.2 = (f32[3,64,512]{2,1,0:T(8,128)S(1)}, f32[3,64,512]{2,1,0:T(8,128)S(1)}, u32[]{:S(2)}, u32[]{:S(2)}) collective-permute-start(f32[3,64,512]{2,1,0:T(8,128)S(1)} %get-tuple-element.626), channel_id=1, source_target_pairs={{0,2},{2,4},{4,6},{6,8},{8,10},{10,12},{12,14},{14,16},{16,18},{18... | collective-permute-start | bytes 1179656 | tf_op jit(solution)/shard_map/ppermute | solution.py:16
  271.6 16.0 %collective-permute-done.2 = f32[3,64,512]{2,1,0:T(8,128)S(1)} collective-permute-done((f32[3,64,512]{2,1,0:T(8,128)S(1)}, f32[3,64,512]{2,1,0:T(8,128)S(1)}, u32[]{:S(2)}, u32[]{:S(2)}) %collective-permute-start.2) | collective-permute-done | bytes 393248 | tf_op jit(solution)/shard_map/ppermute | solution.py:16
  (128 shorter events, 100.1 us)
Async XLA Ops:
  6.5 124.6 %all-reduce.2.cloned.1.call-start = ((), (), s32[]{:S(2)}) async-start(), calls=%async_computation.1 | async-start | bytes 1572864 | tf_op jit(solution)/shard_map/psum | solution.py:74
  7.8 27.2 %collective-permute-start = (f32[2,128,512]{1,2,0:T(8,128)S(1)}, f32[2,128,512]{1,2,0:T(8,128)S(1)}, u32[]{:S(2)}, u32[]{:S(2)}) collective-permute-start(f32[2,128,512]{1,2,0:T(8,128)S(1)} %copy.53), channel_id=1, source_target_pairs={{0,2},{2,4},{4,6},{6,8},{8,10},{10,12},{12,14},{14,16},{16,18},{18... | collective-permute-start | bytes 1572872 | tf_op jit(solution)/shard_map/ppermute | solution.py:16
  12.7 24.4 %collective-permute-start.1 = (f32[2,128,512]{1,2,0:T(8,128)S(1)}, f32[2,128,512]{1,2,0:T(8,128)}, u32[]{:S(2)}, u32[]{:S(2)}) collective-permute-start(f32[2,128,512]{1,2,0:T(8,128)S(1)} %copy.53), channel_id=1, source_target_pairs={{2,0},{4,2},{6,4},{8,6},{10,8},{12,10},{14,12},{16,14},{18,16},{20... | collective-permute-start | bytes 1572872 | tf_op jit(solution)/shard_map/ppermute | solution.py:17
  16.7 1.0 copy-start.1
  19.3 20.1 %copy-start.6 = (s32[3]{0:T(128)S(1)}, s32[3]{0:T(128)}, u32[]{:S(2)}) copy-start(s32[3]{0:T(128)} %param.13) | copy-start | bytes 40
  19.3 20.1 %copy-start.7 = (s32[3]{0:T(128)S(1)}, s32[3]{0:T(128)}, u32[]{:S(2)}) copy-start(s32[3]{0:T(128)} %param.14) | copy-start | bytes 40
  106.9 4.6 %copy-start.3 = (f32[2,4,256,256]{3,2,1,0:T(8,128)S(1)}, f32[2,4,256,256]{3,2,1,0:T(8,128)}, u32[]{:S(2)}) copy-start(f32[2,4,256,256]{3,2,1,0:T(8,128)} %param.11) | copy-start | bytes 6291460
  111.5 19.7 %copy-start.5 = (f32[3,256,256]{2,1,0:T(8,128)S(1)}, f32[3,256,256]{2,1,0:T(8,128)}, u32[]{:S(2)}) copy-start(f32[3,256,256]{2,1,0:T(8,128)} %param.12) | copy-start | bytes 2359300
  111.5 154.0 %reduce-scatter.2.cloned.1.call-start = ((), (), s32[]{:S(2)}) async-start(), calls=%async_computation.2 | async-start | bytes 3538944 | tf_op jit(solution)/shard_map/reduce_scatter | solution.py:110
  147.0 3.7 %copy-start = (bf16[4,256,256]{1,2,0:T(8,128)(2,1)S(1)}, bf16[4,256,256]{1,2,0:T(8,128)(2,1)}, u32[]{:S(2)}) copy-start(bf16[4,256,256]{1,2,0:T(8,128)(2,1)} %fusion.263) | copy-start | bytes 1572868 | tf_op jit(solution)/shard_map/while
  155.7 8.7 %copy-start.2 = (f32[256,256]{1,0:T(8,128)S(1)}, f32[256,256]{1,0:T(8,128)}, u32[]{:S(2)}) copy-start(f32[256,256]{1,0:T(8,128)} %get-tuple-element.895) | copy-start | bytes 786436 | tf_op jit(solution)/shard_map/while
  186.9 3.7 %copy-start = (bf16[4,256,256]{1,2,0:T(8,128)(2,1)S(1)}, bf16[4,256,256]{1,2,0:T(8,128)(2,1)}, u32[]{:S(2)}) copy-start(bf16[4,256,256]{1,2,0:T(8,128)(2,1)} %fusion.263) | copy-start | bytes 1572868 | tf_op jit(solution)/shard_map/while
  195.6 8.7 %copy-start.2 = (f32[256,256]{1,0:T(8,128)S(1)}, f32[256,256]{1,0:T(8,128)}, u32[]{:S(2)}) copy-start(f32[256,256]{1,0:T(8,128)} %get-tuple-element.895) | copy-start | bytes 786436 | tf_op jit(solution)/shard_map/while
  226.4 3.7 %copy-start = (bf16[4,256,256]{1,2,0:T(8,128)(2,1)S(1)}, bf16[4,256,256]{1,2,0:T(8,128)(2,1)}, u32[]{:S(2)}) copy-start(bf16[4,256,256]{1,2,0:T(8,128)(2,1)} %fusion.263) | copy-start | bytes 1572868 | tf_op jit(solution)/shard_map/while
  235.1 8.7 %copy-start.2 = (f32[256,256]{1,0:T(8,128)S(1)}, f32[256,256]{1,0:T(8,128)}, u32[]{:S(2)}) copy-start(f32[256,256]{1,0:T(8,128)} %get-tuple-element.895) | copy-start | bytes 786436 | tf_op jit(solution)/shard_map/while
  254.2 36.5 %copy-start.4 = (f32[2,128,512]{2,1,0:T(8,128)S(1)}, f32[2,128,512]{2,1,0:T(8,128)}, u32[]{:S(2)}) copy-start(f32[2,128,512]{2,1,0:T(8,128)} %param.10) | copy-start | bytes 1572868
  266.7 20.9 %collective-permute-start.2 = (f32[3,64,512]{2,1,0:T(8,128)S(1)}, f32[3,64,512]{2,1,0:T(8,128)S(1)}, u32[]{:S(2)}, u32[]{:S(2)}) collective-permute-start(f32[3,64,512]{2,1,0:T(8,128)S(1)} %get-tuple-element.626), channel_id=1, source_target_pairs={{0,2},{2,4},{4,6},{6,8},{8,10},{10,12},{12,14},{14,16},{16,18},{18... | collective-permute-start | bytes 1179656 | tf_op jit(solution)/shard_map/ppermute | solution.py:16
  270.3 19.2 %collective-permute-start.3 = (f32[3,64,512]{2,1,0:T(8,128)S(1)}, f32[3,64,512]{2,1,0:T(8,128)S(1)}, u32[]{:S(2)}, u32[]{:S(2)}) collective-permute-start(f32[3,64,512]{2,1,0:T(8,128)S(1)} %get-tuple-element.627), channel_id=1, source_target_pairs={{2,0},{4,2},{6,4},{8,6},{10,8},{12,10},{14,12},{16,14},{18,16},{20... | collective-permute-start | bytes 1179656 | tf_op jit(solution)/shard_map/ppermute | solution.py:17
Sparse Core Ops, SparseCore 0:
  111.6 19.5 all-reduce.1
  254.3 11.1 reduce-scatter.1
where the time goes:
time: 300 us; the launch traced here: 298 us
  matrix products  91.6 us (31%)
  waiting for transfers between devices  65.7 us (22%)
  local copies, waits for them, and re-layouts  65.3 us (22%)
  loops' own time  29.5 us (10%)
  other arithmetic  21.5 us (7%)
  between operations  13.6 us (5%)
  starting transfers between devices  11.1 us (4%)
    dot_general x24, matrix products, right_product(): jnp.einsum('kub,bv->kuv', stacked, table, preferred_element_type=jnp.floa...  52.4 us
    dot_general x24, matrix products, left_product(): jnp.einsum('ua,kab->kub', table, stacked, preferred_element_type=jnp.floa...  39.2 us
    ppermute x2, waiting for transfers between devices, extended_2(): before = lax.ppermute(last, axis, up)  31.6 us
    dynamic_update_slice x3, local copies, waits for them, and re-layouts, backward(): return lax.dynamic_update_slice(buffer, current + contrib, corner)  26.9 us
    psum x1, waiting for transfers between devices, local(): model_power = lax.psum(power_sum, 'mode')  18.8 us
    another operation x1, loops' own time, local(): lax.map(forward, jnp.arange(slot_count, dtype=jnp.int32))  17 us
    another operation x1, loops' own time, local(): lax.fori_loop(0, slot_count, backward, jnp.zeros((3, 3 * rows_tile, colum...  12.5 us
    reduce_scatter x1, waiting for transfers between devices, local(): shared = lax.psum_scatter(blocked, 'mode', scatter_dimension=2, tiled=True)  11.3 us
  transfers between devices with their start and end apart: 6, of which 6 were waited for; matrix products, arithmetic and copies ran while one was open for 2% of the time, Pallas kernels for 0%

commit v1 on v0

v1 whole, which is shorter than its diff:
```python
import functools
import math

import jax
import jax.numpy as jnp
import numpy as np
from jax import lax
from jax.experimental import pallas as pl
from jax.experimental.pallas import tpu as pltpu
from jax.sharding import PartitionSpec as P

MESH = pl.DeviceIdType.MESH


def dft_tables(pattern):
    counter = np.arange(pattern)
    angles = (counter[:, None] * counter[None, :] % pattern) * (2.0 * math.pi / pattern)
    factor = 1.0 / math.sqrt(pattern)
    real = (np.cos(angles) * factor).astype(np.float32)
    imag = (-np.sin(angles) * factor).astype(np.float32)
    plain = np.block([[real, -imag], [imag, real]]).astype(jnp.bfloat16)
    turned = np.block([[real, imag], [-imag, real]]).astype(jnp.bfloat16)
    return plain, turned


def kernel(
    n, nm, chunks,
    row_ref, col_ref, count_ref, obj_ref, probe_ref, meas_ref, plain_ref, turned_ref,
    out_ref,
    ext, acc, illum, exit_ref, wave_ref, power, power_in, pp, pp_in, red_in,
    far_out, far_in, near_out, near_in, il_far_in, il_near_out, il_near_in,
    halo_s, halo_r, fwd_s, fwd_r, brn_s, brn_r, brf_s, brf_r,
    pow_s, pow_r, pp_s, pp_r, ilf_s, ilf_r, iln_s, iln_r,
    red_s, red_r, rf_s, rf_r, rn_s, rn_r,
):
    tile, cols = obj_ref.shape[1], obj_ref.shape[2]
    slots, pat = meas_ref.shape[0], meas_ref.shape[1]
    modes = probe_ref.shape[1]
    share = tile // nm
    piece = share // chunks
    lift = tile - pat // 2

    p = lax.axis_index("pos")
    m = lax.axis_index("mode")
    odd = lax.rem(p, 2)
    near_dev = p + 1 - 2 * odd
    far_blk = 2 * odd
    near_blk = 2 - far_blk
    far_raw = p - 2 + 4 * odd
    back_raw = p + 2 - 4 * odd
    has_far = jnp.logical_and(far_raw >= 0, far_raw < n)
    has_back = jnp.logical_and(back_raw >= 0, back_raw < n)
    far_dev = lax.rem(far_raw + n, n)
    back_dev = lax.rem(back_raw + n, n)
    others = [lax.rem(m + j, nm) for j in range(1, nm)]

    def rows_of(block, mode, c=0, size=None):
        size = share if size is None else size
        return pl.ds(pl.multiple_of(block * tile + mode * share + c * piece, 8), size)

    def remote(src, dst, s, r, pos, mode):
        return pltpu.make_async_remote_copy(
            src_ref=src, dst_ref=dst, send_sem=s, recv_sem=r,
            device_id=(pos, mode), device_id_type=MESH,
        )

    barrier = pltpu.get_barrier_semaphore()
    pl.semaphore_signal(barrier, inc=1, device_id=(near_dev, m), device_id_type=MESH)
    for other in others:
        pl.semaphore_signal(barrier, inc=1, device_id=(p, other), device_id_type=MESH)

    @pl.when(has_far)
    def _():
        pl.semaphore_signal(barrier, inc=1, device_id=(far_dev, m), device_id_type=MESH)

    @pl.when(has_back)
    def _():
        pl.semaphore_signal(barrier, inc=1, device_id=(back_dev, m), device_id_type=MESH)

    greeted = has_far.astype(jnp.int32) + has_back.astype(jnp.int32)
    pl.semaphore_wait(barrier, nm + greeted)

    def halo(c):
        return remote(
            obj_ref.at[:, rows_of(0, m, c, piece), :], ext.at[:, rows_of(far_blk, m, c, piece), :],
            halo_s.at[c], halo_r.at[c], near_dev, m,
        )

    def forward_near(c):
        return remote(
            ext.at[:, rows_of(near_blk, m, c, piece), :],
            ext.at[:, rows_of(far_blk, m, c, piece), :],
            fwd_s.at[c], fwd_r.at[c], back_dev, m,
        )

    def spread(block, c, j, s, r):
        where = rows_of(block, m, c, piece)
        return remote(
            ext.at[:, where, :], ext.at[:, where, :], s.at[j, c], r.at[j, c], p, others[j]
        )

    for c in range(chunks):
        halo(c).start()

    total = jnp.zeros((pat, pat), jnp.float32)
    for k in range(modes):
        total = total + probe_ref[0, k] * probe_ref[0, k] + probe_ref[1, k] * probe_ref[1, k]
    pp[...] = total

    def pp_copy(j):
        return remote(pp, pp_in.at[j], pp_s.at[j], pp_r.at[j], p, others[j])

    for j in range(nm - 1):
        pp_copy(j).start()

    ext[:, tile : 2 * tile, :] = obj_ref[...]
    acc[...] = jnp.zeros_like(acc)
    illum[...] = jnp.zeros_like(illum)

    @pl.when(jnp.logical_not(has_far))
    def _():
        ext[:, pl.ds(pl.multiple_of(far_blk * tile, 8), tile), :] = jnp.zeros(
            (2, tile, cols), jnp.float32
        )

    for c in range(chunks):
        halo(c).wait_recv()

        @pl.when(has_back)
        def _():
            forward_near(c).start()

        for j in range(nm - 1):
            spread(near_blk, c, j, brn_s, brn_r).start()

    for j in range(nm - 1):
        pp_copy(j).wait_recv()

    live = count_ref[0]

    steps = []
    while sum(steps) < (3 * tile - pat) // 8 - 1:
        steps.insert(0, max(1, 2 * sum(steps[:1])))

    def placed(values, slot):
        top = lift + row_ref[slot]
        by = lax.rem(top, 8)
        groups = lax.div(top, 8)
        turned_rows = pltpu.roll(values.reshape(pat // 8, 8, pat), by, 1)
        blank = jnp.zeros((1, 8, pat), jnp.float32)
        upper = jnp.concatenate([turned_rows, blank], axis=0)
        lower = jnp.concatenate([blank, turned_rows], axis=0)
        line = lax.broadcasted_iota(jnp.int32, (1, 8, pat), 1)
        values = jnp.where(line >= by, upper, lower).reshape(pat + 8, pat)
        wide = jnp.concatenate([values, jnp.zeros((pat + 8, cols - pat), jnp.float32)], axis=1)
        wide = pltpu.roll(wide, col_ref[slot], 1).reshape(pat // 8 + 1, 8, cols)
        for step in reversed(steps):
            blank = jnp.zeros((step, 8, cols), jnp.float32)
            far = lax.rem(lax.div(groups, step), 2) == 1
            wide = jnp.where(
                far,
                jnp.concatenate([blank, wide], axis=0),
                jnp.concatenate([wide, blank], axis=0),
            )
        return wide.reshape(3 * tile, cols)

    def window(part, slot):
        top = lift + row_ref[slot]
        by = lax.rem(top, 8)
        groups = lax.div(top, 8)
        rows = ext[part].reshape(3 * tile // 8, 8, cols)
        for step in steps:
            far = lax.rem(lax.div(groups, step), 2) == 1
            rows = jnp.where(far, rows[step:], rows[:-step])
        turn = lax.rem(cols - col_ref[slot], cols)
        rows = pltpu.roll(rows.reshape(pat + 8, cols), turn, 1)
        rows = rows[:, :pat].reshape(pat // 8 + 1, 8, pat)
        rows = pltpu.roll(rows, lax.rem(8 - by, 8), 1)
        line = lax.broadcasted_iota(jnp.int32, (1, 8, pat), 1)
        return jnp.where(line < 8 - by, rows[:-1], rows[1:]).reshape(pat, pat)

    def add_illum(s, carry):
        whole = pp[...]
        for j in range(nm - 1):
            whole = whole + pp_in[j]
        whole = jnp.where(s < live, whole, 0.0)
        illum[...] += placed(whole, s)
        return carry

    lax.fori_loop(0, slots, add_illum, 0)

    @pl.when(has_far)
    def _():
        for c in range(chunks):
            forward_near(c).wait_recv()
            for j in range(nm - 1):
                spread(far_blk, c, j, brf_s, brf_r).start()

    def illum_far():
        return remote(
            illum.at[rows_of(far_blk, m), :], il_far_in, ilf_s.at[0], ilf_r.at[0], far_dev, m
        )

    def illum_near():
        return remote(il_near_out, il_near_in, iln_s.at[0], iln_r.at[0], near_dev, m)

    @pl.when(has_far)
    def _():
        illum_far().start()

    for c in range(chunks):
        for j in range(nm - 1):
            spread(near_blk, c, j, brn_s, brn_r).wait_recv()

    @pl.when(has_far)
    def _():
        for c in range(chunks):
            for j in range(nm - 1):
                spread(far_blk, c, j, brf_s, brf_r).wait_recv()

    def power_copy(s, j):
        return remote(
            power.at[s], power_in.at[s, j], pow_s.at[s, j], pow_r.at[s, j], p, others[j]
        )

    def forward(s, carry):
        win_re = window(0, s)
        win_im = window(1, s)
        model = jnp.zeros((pat, pat), jnp.float32)
        for k in range(modes):
            probe_re, probe_im = probe_ref[0, k], probe_ref[1, k]
            exit_re = (probe_re * win_re - probe_im * win_im).astype(jnp.bfloat16)
            exit_im = (probe_re * win_im + probe_im * win_re).astype(jnp.bfloat16)
            stacked = jnp.concatenate([exit_re, exit_im], axis=0)
            exit_ref[s, k] = stacked
            half = jnp.dot(plain_ref[...], stacked, preferred_element_type=jnp.float32)
            half = half.astype(jnp.bfloat16)
            half = jnp.concatenate([half[:pat], half[pat:]], axis=1)
            wave = jnp.dot(half, turned_ref[...], preferred_element_type=jnp.float32)
            wave_ref[s, k] = wave
            model = model + wave[:, :pat] * wave[:, :pat] + wave[:, pat:] * wave[:, pat:]
        power[s] = model
        for j in range(nm - 1):
            power_copy(s, j).start()
        return carry

    lax.fori_loop(0, slots, forward, 0)

    @pl.when(has_back)
    def _():
        illum_far().wait_recv()
        il_near_out[...] = illum[rows_of(near_blk, m), :] + il_far_in[...]

    @pl.when(jnp.logical_not(has_back))
    def _():
        il_near_out[...] = illum[rows_of(near_blk, m), :]

    illum_near().start()

    def backward(s, carry):
        model = power[s]
        for j in range(nm - 1):
            power_copy(s, j).wait_recv()
            model = model + power_in[s, j]
        scaling = jnp.sqrt(meas_ref[s]) / jnp.maximum(jnp.sqrt(model), 1.0)
        numer_re = jnp.zeros((pat, pat), jnp.float32)
        numer_im = jnp.zeros((pat, pat), jnp.float32)
        for k in range(modes):
            fixed_re = (scaling * wave_ref[s, k, :, :pat]).astype(jnp.bfloat16)
            fixed_im = (scaling * wave_ref[s, k, :, pat:]).astype(jnp.bfloat16)
            fixed = jnp.concatenate([fixed_re, fixed_im], axis=0)
            back = jnp.dot(turned_ref[...], fixed, preferred_element_type=jnp.float32)
            back = back.astype(jnp.bfloat16)
            back = jnp.concatenate([back[:pat], back[pat:]], axis=1)
            delta = jnp.dot(back, plain_ref[...], preferred_element_type=jnp.float32)
            delta_re = delta[:, :pat] - exit_ref[s, k, :pat, :].astype(jnp.float32)
            delta_im = delta[:, pat:] - exit_ref[s, k, pat:, :].astype(jnp.float32)
            probe_re, probe_im = probe_ref[0, k], probe_ref[1, k]
            numer_re = numer_re + probe_re * delta_re + probe_im * delta_im
            numer_im = numer_im + probe_re * delta_im - probe_im * delta_re
        on = s < live
        acc[0] += placed(jnp.where(on, numer_re, 0.0), s)
        acc[1] += placed(jnp.where(on, numer_im, 0.0), s)
        return carry

    lax.fori_loop(0, slots, backward, 0)

    blocks = (far_blk, near_blk, 1)

    def reduce_copy(b, j):
        return remote(
            acc.at[:, rows_of(blocks[b], others[j]), :], red_in.at[j, b],
            red_s.at[j, b], red_r.at[j, b], p, others[j],
        )

    for b in range(3):
        for j in range(nm - 1):
            reduce_copy(b, j).start()

    def reduced(b):
        value = acc[:, rows_of(blocks[b], m), :]
        for j in range(nm - 1):
            reduce_copy(b, j).wait_recv()
            value = value + red_in[j, b]
        return value

    def far_copy(c):
        part = pl.ds(c * piece, piece)
        return remote(
            far_out.at[:, part, :], far_in.at[:, part, :], rf_s.at[c], rf_r.at[c], far_dev, m
        )

    def near_copy(c):
        part = pl.ds(c * piece, piece)
        return remote(
            near_out.at[:, part, :], near_in.at[:, part, :], rn_s.at[c], rn_r.at[c], near_dev, m
        )

    far_out[...] = reduced(0)

    @pl.when(has_far)
    def _():
        for c in range(chunks):
            far_copy(c).start()

    near_out[...] = reduced(1)
    for c in range(chunks):

        @pl.when(has_back)
        def _():
            part = pl.ds(c * piece, piece)
            far_copy(c).wait_recv()
            near_out[:, part, :] = near_out[:, part, :] + far_in[:, part, :]

        near_copy(c).start()

    own_sum = reduced(2)
    illum_near().wait_recv()
    weight = 1.0 / (illum[rows_of(1, m), :] + il_near_in[...] + 1.0)
    for c in range(chunks):
        near_copy(c).wait_recv()
        part = slice(c * piece, (c + 1) * piece)
        out_ref[:, part, :] = obj_ref[:, rows_of(0, m, c, piece), :] + (
            own_sum[:, part] + near_in[:, part, :]
        ) * weight[part]

    for c in range(chunks):
        halo(c).wait_send()
        near_copy(c).wait_send()
        for j in range(nm - 1):
            spread(near_blk, c, j, brn_s, brn_r).wait_send()
    for j in range(nm - 1):
        pp_copy(j).wait_send()
        for s in range(slots):
            power_copy(s, j).wait_send()
        for b in range(3):
            reduce_copy(b, j).wait_send()
    illum_near().wait_send()

    @pl.when(has_far)
    def _():
        illum_far().wait_send()
        for c in range(chunks):
            far_copy(c).wait_send()
            for j in range(nm - 1):
                spread(far_blk, c, j, brf_s, brf_r).wait_send()

    @pl.when(has_back)
    def _():
        for c in range(chunks):
            forward_near(c).wait_send()


def local(object_field, probe, measured, row_offsets, col_offsets, tile_counts):
    n, nm = lax.axis_size("pos"), lax.axis_size("mode")
    tile, cols = object_field.shape[1:]
    slots, pat = measured.shape[:2]
    modes = probe.shape[1]
    share = tile // nm
    chunks = min(4, share // 8)
    plain, turned = dft_tables(pat)
    f32, bf16 = jnp.float32, jnp.bfloat16
    vmem = pl.BlockSpec(memory_space=pltpu.VMEM)
    smem = pl.BlockSpec(memory_space=pltpu.SMEM)
    dma = pltpu.SemaphoreType.DMA
    others = nm - 1
    scratch = [
        pltpu.VMEM((2, 3 * tile, cols), f32),
        pltpu.VMEM((2, 3 * tile, cols), f32),
        pltpu.VMEM((3 * tile, cols), f32),
        pltpu.VMEM((slots, modes, 2 * pat, pat), bf16),
        pltpu.VMEM((slots, modes, pat, 2 * pat), f32),
        pltpu.VMEM((slots, pat, pat), f32),
        pltpu.VMEM((slots, others, pat, pat), f32),
        pltpu.VMEM((pat, pat), f32),
        pltpu.VMEM((others, pat, pat), f32),
        pltpu.VMEM((others, 3, 2, share, cols), f32),
        pltpu.VMEM((2, share, cols), f32),
        pltpu.VMEM((2, share, cols), f32),
        pltpu.VMEM((2, share, cols), f32),
        pltpu.VMEM((2, share, cols), f32),
        pltpu.VMEM((share, cols), f32),
        pltpu.VMEM((share, cols), f32),
        pltpu.VMEM((share, cols), f32),
        dma((chunks,)), dma((chunks,)), dma((chunks,)), dma((chunks,)),
        dma((others, chunks)), dma((others, chunks)), dma((others, chunks)), dma((others, chunks)),
        dma((slots, others)), dma((slots, others)), dma((others,)), dma((others,)),
        dma((1,)), dma((1,)), dma((1,)), dma((1,)),
        dma((others, 3)), dma((others, 3)),
        dma((chunks,)), dma((chunks,)), dma((chunks,)), dma((chunks,)),
    ]
    return pl.pallas_call(
        functools.partial(kernel, n, nm, chunks),
        out_shape=jax.ShapeDtypeStruct((2, share, cols), f32),
        in_specs=[smem] * 3 + [vmem] * 5,
        out_specs=vmem,
        scratch_shapes=scratch,
        compiler_params=pltpu.CompilerParams(
            collective_id=0, has_side_effects=True, vmem_limit_bytes=48 * 1024 * 1024
        ),
    )(
        row_offsets, col_offsets, tile_counts, object_field, probe, measured,
        jnp.asarray(plain), jnp.asarray(turned),
    )


def solution(mesh):
    in_specs = (
        P(None, "pos", None),
        P(None, "mode", None, None),
        P("pos", None, None),
        P("pos"),
        P("pos"),
        P("pos"),
    )
    out_specs = P(None, ("pos", "mode"), None)
    return jax.shard_map(local, mesh=mesh, in_specs=in_specs, out_specs=out_specs, check_vma=False)
```

time: 300 us -> 48.7 us (0.16)
  matrix products: 91.6 us -> 0 us
  waiting for transfers between devices: 65.7 us -> 0 us
  local copies, waits for them, and re-layouts: 65.3 us -> 7.85 us
  Pallas kernels: 0 us -> 39.4 us
  loops' own time: 29.5 us -> 0 us
  other arithmetic: 21.5 us -> 0 us
  between operations: 13.6 us -> 0.67 us
  starting transfers between devices: 11.1 us -> 0 us
    dot_general x48 -> x0, matrix products: 91.6 us -> none  [the longest x24 52.4 us: right_product(): jnp.einsum('kub,bv->kuv', stacked, table, preferred_element_type=jnp.floa...]
    pallas_call x0 -> x1, Pallas kernels: none -> 39.4 us  [local(): pl.pallas_call(functools.partial(kernel, n, nm, chunks), out_shape=jax.Sh...]
    ppermute x4 -> x0, waiting for transfers between devices: 35.6 us -> none  [the longest x2 31.6 us: extended_2(): before = lax.ppermute(last, axis, up)]
    another operation x2 -> x0, loops' own time: 29.5 us -> none  [the longest x1 17 us: local(): lax.map(forward, jnp.arange(slot_count, dtype=jnp.int32))]
    dynamic_update_slice x3 -> x0, local copies, waits for them, and re-layouts: 26.9 us -> none  [backward(): return lax.dynamic_update_slice(buffer, current + contrib, corner)]
    dynamic_slice x39 -> x0, local copies, waits for them, and re-layouts: 24.8 us -> none  [the longest x6 6.28 us: backward(): fixed_im = (scaling[position] * wave_im[position]).astype(jnp.bfloat16)]
    psum x1 -> x0, waiting for transfers between devices: 18.8 us -> none  [local(): model_power = lax.psum(power_sum, 'mode')]
    reduce_scatter x1 -> x0, waiting for transfers between devices: 11.3 us -> none  [local(): shared = lax.psum_scatter(blocked, 'mode', scatter_dimension=2, tiled=True)]
  transfers between devices with their start and end apart: 6 -> 0, of which waited for: 6 -> 0; matrix products, arithmetic and copies ran while one was open for 2% -> 0% of each run, Pallas kernels for 0% -> 0%
where the time goes in v1:
time: 48.7 us; the launch traced here: 47.9 us
  Pallas kernels  39.4 us (81%)
  local copies, waits for them, and re-layouts  7.85 us (16%)
  between operations  0.67 us (1%)
    pallas_call x1, Pallas kernels, local(): pl.pallas_call(functools.partial(kernel, n, nm, chunks), out_shape=jax.Sh...  39.4 us
    unnamed x15, local copies, waits for them, and re-layouts  7.85 us

profile of v1, /device:TPU:0, one launch (start us, length us, event | category | flops | bytes accessed | tf_op | source)
XLA Modules:
  0.0 47.9 jit_solution(11114930864202567410)
XLA Ops:
  0.7 0.0 copy-start
  0.7 1.6 %copy-done = f32[2,4,256,256]{3,2,1,0:T(8,128)S(1)} copy-done((f32[2,4,256,256]{3,2,1,0:T(8,128)S(1)}, f32[2,4,256,256]{3,2,1,0:T(8,128)}, u32[]{:S(2)}) %copy-start) | copy-done | bytes 2097176
  2.2 0.0 copy-start.1
  2.2 1.1 %copy-done.1 = f32[3,256,256]{2,1,0:T(8,128)S(1)} copy-done((f32[3,256,256]{2,1,0:T(8,128)S(1)}, f32[3,256,256]{2,1,0:T(8,128)}, u32[]{:S(2)}) %copy-start.1) | copy-done | bytes 786456
  3.4 0.0 copy-start.2
  3.4 1.0 %copy-done.2 = f32[2,128,512]{2,1,0:T(8,128)S(1)} copy-done((f32[2,128,512]{2,1,0:T(8,128)S(1)}, f32[2,128,512]{2,1,0:T(8,128)}, u32[]{:S(2)}) %copy-start.2) | copy-done | bytes 524312
  4.4 0.0 copy-start.3
  4.4 1.0 %copy-done.3 = bf16[512,512]{1,0:T(8,128)(2,1)S(1)} copy-done((bf16[512,512]{1,0:T(8,128)(2,1)S(1)}, bf16[512,512]{1,0:T(8,128)(2,1)}, u32[]{:S(2)}) %copy-start.3) | copy-done | bytes 524312
  5.5 0.0 copy-start.4
  5.5 1.0 %copy-done.4 = bf16[512,512]{1,0:T(8,128)(2,1)S(1)} copy-done((bf16[512,512]{1,0:T(8,128)(2,1)S(1)}, bf16[512,512]{1,0:T(8,128)(2,1)}, u32[]{:S(2)}) %copy-start.4) | copy-done | bytes 524312
  6.5 0.0 copy-start.5
  6.5 0.7 %copy-done.5 = s32[3]{0:T(128)S(1)} copy-done((s32[3]{0:T(128)S(1)}, s32[3]{0:T(128)}, u32[]{:S(2)}) %copy-start.5) | copy-done | bytes 36
  7.2 0.0 copy-start.6
  7.2 0.7 %copy-done.6 = s32[3]{0:T(128)S(1)} copy-done((s32[3]{0:T(128)S(1)}, s32[3]{0:T(128)}, u32[]{:S(2)}) %copy-start.6) | copy-done | bytes 36
  7.8 39.4 %shard_map.82 = f32[2,64,512]{2,1,0:T(8,128)S(1)} custom-call(s32[3]{0:T(128)S(1)} %copy-done.5, s32[3]{0:T(128)S(1)} %copy-done.6, s32[1]{0:T(128)S(6)} %copy.10.count_ref, f32[2,128,512]{2,1,0:T(8,128)S(1)} %copy-done.2, f32[2,4,256,256]{3,2,1,0:T(8,128)S(1)} %copy-done, f32[3,256,256]{2,1,0:T(8,128)S(1)} %copy-done.1, bf16[512,512]{1,0:T(8,128)(2,1)S(1)} %copy-done.4, ...), custom_call_target="tpu_custom_call" | custom-call | tf_op jit(solution)/shard_map/pallas_call | solution.py:412
  47.2 0.7 %copy.11 = f32[2,64,512]{2,1,0:T(8,128)} copy(f32[2,64,512]{2,1,0:T(8,128)S(1)} %shard_map.82) | data formatting | bytes 524288
Async XLA Ops:
  0.7 1.6 %copy-start = (f32[2,4,256,256]{3,2,1,0:T(8,128)S(1)}, f32[2,4,256,256]{3,2,1,0:T(8,128)}, u32[]{:S(2)}) copy-start(f32[2,4,256,256]{3,2,1,0:T(8,128)} %probe_ref.1) | copy-start | bytes 6291460
  2.2 1.1 %copy-start.1 = (f32[3,256,256]{2,1,0:T(8,128)S(1)}, f32[3,256,256]{2,1,0:T(8,128)}, u32[]{:S(2)}) copy-start(f32[3,256,256]{2,1,0:T(8,128)} %meas_ref.1) | copy-start | bytes 2359300
  3.4 1.0 %copy-start.2 = (f32[2,128,512]{2,1,0:T(8,128)S(1)}, f32[2,128,512]{2,1,0:T(8,128)}, u32[]{:S(2)}) copy-start(f32[2,128,512]{2,1,0:T(8,128)} %obj_ref.1) | copy-start | bytes 1572868
  4.4 1.0 %copy-start.3 = (bf16[512,512]{1,0:T(8,128)(2,1)S(1)}, bf16[512,512]{1,0:T(8,128)(2,1)}, u32[]{:S(2)}) copy-start(bf16[512,512]{1,0:T(8,128)(2,1)} %constant.5.clone.turned_ref) | copy-start | bytes 1572868
  5.5 1.0 %copy-start.4 = (bf16[512,512]{1,0:T(8,128)(2,1)S(1)}, bf16[512,512]{1,0:T(8,128)(2,1)}, u32[]{:S(2)}) copy-start(bf16[512,512]{1,0:T(8,128)(2,1)} %constant.4.clone.plain_ref) | copy-start | bytes 1572868
  6.5 0.7 %copy-start.5 = (s32[3]{0:T(128)S(1)}, s32[3]{0:T(128)}, u32[]{:S(2)}) copy-start(s32[3]{0:T(128)} %row_ref.1) | copy-start | bytes 40
  7.2 0.7 %copy-start.6 = (s32[3]{0:T(128)S(1)}, s32[3]{0:T(128)}, u32[]{:S(2)}) copy-start(s32[3]{0:T(128)} %col_ref.1) | copy-start | bytes 40

commit v2 on v1

--- a/solution.py
+++ b/solution.py
@@ -25,15 +25,16 @@
 
 def kernel(
     n, nm, chunks,
-    row_ref, col_ref, count_ref, obj_ref, probe_ref, meas_ref, plain_ref, turned_ref,
+    row_hbm, col_hbm, count_hbm, obj_hbm, probe_hbm, meas_hbm, plain_hbm, turned_hbm,
     out_ref,
+    row_ref, col_ref, count_ref, probe_ref, meas_ref, plain_ref, turned_ref, load_s,
     ext, acc, illum, exit_ref, wave_ref, power, power_in, pp, pp_in, red_in,
     far_out, far_in, near_out, near_in, il_far_in, il_near_out, il_near_in,
     halo_s, halo_r, fwd_s, fwd_r, brn_s, brn_r, brf_s, brf_r,
     pow_s, pow_r, pp_s, pp_r, ilf_s, ilf_r, iln_s, iln_r,
     red_s, red_r, rf_s, rf_r, rn_s, rn_r,
 ):
-    tile, cols = obj_ref.shape[1], obj_ref.shape[2]
+    tile, cols = obj_hbm.shape[1], obj_hbm.shape[2]
     slots, pat = meas_ref.shape[0], meas_ref.shape[1]
     modes = probe_ref.shape[1]
     share = tile // nm
@@ -64,6 +65,12 @@
             device_id=(pos, mode), device_id_type=MESH,
         )
 
+    own = ext.at[:, tile : 2 * tile, :]
+    pairs = (
+        (probe_hbm, probe_ref), (row_hbm, row_ref), (col_hbm, col_ref), (count_hbm, count_ref),
+        (obj_hbm, own), (plain_hbm, plain_ref), (turned_hbm, turned_ref), (meas_hbm, meas_ref),
+    )
+    loads = [pltpu.make_async_copy(a, b, load_s.at[i]) for i, (a, b) in enumerate(pairs)]
     barrier = pltpu.get_barrier_semaphore()
     pl.semaphore_signal(barrier, inc=1, device_id=(near_dev, m), device_id_type=MESH)
     for other in others:
@@ -78,11 +85,13 @@
         pl.semaphore_signal(barrier, inc=1, device_id=(back_dev, m), device_id_type=MESH)
 
     greeted = has_far.astype(jnp.int32) + has_back.astype(jnp.int32)
+    for load in loads:
+        load.start()
     pl.semaphore_wait(barrier, nm + greeted)
 
     def halo(c):
         return remote(
-            obj_ref.at[:, rows_of(0, m, c, piece), :], ext.at[:, rows_of(far_blk, m, c, piece), :],
+            obj_hbm.at[:, rows_of(0, m, c, piece), :], ext.at[:, rows_of(far_blk, m, c, piece), :],
             halo_s.at[c], halo_r.at[c], near_dev, m,
         )
 
@@ -102,6 +111,7 @@
     for c in range(chunks):
         halo(c).start()
 
+    loads[0].wait()
     total = jnp.zeros((pat, pat), jnp.float32)
     for k in range(modes):
         total = total + probe_ref[0, k] * probe_ref[0, k] + probe_ref[1, k] * probe_ref[1, k]
@@ -113,7 +123,8 @@
     for j in range(nm - 1):
         pp_copy(j).start()
 
-    ext[:, tile : 2 * tile, :] = obj_ref[...]
+    for load in loads[1:]:
+        load.wait()
     acc[...] = jnp.zeros_like(acc)
     illum[...] = jnp.zeros_like(illum)
 
@@ -340,7 +351,7 @@
     for c in range(chunks):
         near_copy(c).wait_recv()
         part = slice(c * piece, (c + 1) * piece)
-        out_ref[:, part, :] = obj_ref[:, rows_of(0, m, c, piece), :] + (
+        out_ref[:, part, :] = ext[:, rows_of(1, m, c, piece), :] + (
             own_sum[:, part] + near_in[:, part, :]
         ) * weight[part]
 
@@ -381,10 +392,18 @@
     plain, turned = dft_tables(pat)
     f32, bf16 = jnp.float32, jnp.bfloat16
     vmem = pl.BlockSpec(memory_space=pltpu.VMEM)
-    smem = pl.BlockSpec(memory_space=pltpu.SMEM)
+    anywhere = pl.BlockSpec(memory_space=pl.ANY)
     dma = pltpu.SemaphoreType.DMA
     others = nm - 1
     scratch = [
+        pltpu.SMEM((slots,), jnp.int32),
+        pltpu.SMEM((slots,), jnp.int32),
+        pltpu.SMEM((1,), jnp.int32),
+        pltpu.VMEM((2, modes, pat, pat), f32),
+        pltpu.VMEM((slots, pat, pat), f32),
+        pltpu.VMEM((2 * pat, 2 * pat), bf16),
+        pltpu.VMEM((2 * pat, 2 * pat), bf16),
+        dma((8,)),
         pltpu.VMEM((2, 3 * tile, cols), f32),
         pltpu.VMEM((2, 3 * tile, cols), f32),
         pltpu.VMEM((3 * tile, cols), f32),
@@ -412,7 +431,7 @@
     return pl.pallas_call(
         functools.partial(kernel, n, nm, chunks),
         out_shape=jax.ShapeDtypeStruct((2, share, cols), f32),
-        in_specs=[smem] * 3 + [vmem] * 5,
+        in_specs=[anywhere] * 8,
         out_specs=vmem,
         scratch_shapes=scratch,
         compiler_params=pltpu.CompilerParams(

time: 48.7 us -> 47.7 us (0.979)
  Pallas kernels: 39.4 us -> 38.4 us
    pallas_call x1, Pallas kernels: 39.4 us -> 38.4 us  [local(): pl.pallas_call(functools.partial(kernel, n, nm, chunks), out_shape=jax.Sh...]
where the time goes in v2:
time: 47.7 us; the launch traced here: 46.9 us
  Pallas kernels  38.4 us (81%)
  local copies, waits for them, and re-layouts  7.85 us (16%)
  between operations  0.67 us (1%)
    pallas_call x1, Pallas kernels, local(): pl.pallas_call(functools.partial(kernel, n, nm, chunks), out_shape=jax.Sh...  38.4 us
    unnamed x15, local copies, waits for them, and re-layouts  7.85 us

profile of v2, /device:TPU:0, one launch (start us, length us, event | category | flops | bytes accessed | tf_op | source)
XLA Modules:
  0.0 46.9 jit_solution(5087969847812564677)
XLA Ops:
  0.7 0.0 copy-start
  0.7 1.6 %copy-done = f32[2,4,256,256]{3,2,1,0:T(8,128)S(1)} copy-done((f32[2,4,256,256]{3,2,1,0:T(8,128)S(1)}, f32[2,4,256,256]{3,2,1,0:T(8,128)}, u32[]{:S(2)}) %copy-start) | copy-done | bytes 2097176
  2.2 0.0 copy-start.1
  2.2 1.1 %copy-done.1 = f32[3,256,256]{2,1,0:T(8,128)S(1)} copy-done((f32[3,256,256]{2,1,0:T(8,128)S(1)}, f32[3,256,256]{2,1,0:T(8,128)}, u32[]{:S(2)}) %copy-start.1) | copy-done | bytes 786456
  3.4 0.0 copy-start.2
  3.4 1.0 %copy-done.2 = f32[2,128,512]{2,1,0:T(8,128)S(1)} copy-done((f32[2,128,512]{2,1,0:T(8,128)S(1)}, f32[2,128,512]{2,1,0:T(8,128)}, u32[]{:S(2)}) %copy-start.2) | copy-done | bytes 524312
  4.4 0.0 copy-start.3
  4.4 1.0 %copy-done.3 = bf16[512,512]{1,0:T(8,128)(2,1)S(1)} copy-done((bf16[512,512]{1,0:T(8,128)(2,1)S(1)}, bf16[512,512]{1,0:T(8,128)(2,1)}, u32[]{:S(2)}) %copy-start.3) | copy-done | bytes 524312
  5.5 0.0 copy-start.4
  5.5 1.0 %copy-done.4 = bf16[512,512]{1,0:T(8,128)(2,1)S(1)} copy-done((bf16[512,512]{1,0:T(8,128)(2,1)S(1)}, bf16[512,512]{1,0:T(8,128)(2,1)}, u32[]{:S(2)}) %copy-start.4) | copy-done | bytes 524312
  6.5 0.0 copy-start.5
  6.5 0.7 %copy-done.5 = s32[3]{0:T(128)S(1)} copy-done((s32[3]{0:T(128)S(1)}, s32[3]{0:T(128)}, u32[]{:S(2)}) %copy-start.5) | copy-done | bytes 36
  7.2 0.0 copy-start.6
  7.2 0.7 %copy-done.6 = s32[3]{0:T(128)S(1)} copy-done((s32[3]{0:T(128)S(1)}, s32[3]{0:T(128)}, u32[]{:S(2)}) %copy-start.6) | copy-done | bytes 36
  7.8 38.4 %shard_map.82 = f32[2,64,512]{2,1,0:T(8,128)S(1)} custom-call(s32[3]{0:T(128)S(1)} %copy-done.5, s32[3]{0:T(128)S(1)} %copy-done.6, s32[1]{0:T(128)S(6)} %copy.10.count_hbm, f32[2,128,512]{2,1,0:T(8,128)S(1)} %copy-done.2, f32[2,4,256,256]{3,2,1,0:T(8,128)S(1)} %copy-done, f32[3,256,256]{2,1,0:T(8,128)S(1)} %copy-done.1, bf16[512,512]{1,0:T(8,128)(2,1)S(1)} %copy-done.4, ...), custom_call_target="tpu_custom_call" | custom-call | tf_op jit(solution)/shard_map/pallas_call | solution.py:431
  46.2 0.7 %copy.11 = f32[2,64,512]{2,1,0:T(8,128)} copy(f32[2,64,512]{2,1,0:T(8,128)S(1)} %shard_map.82) | data formatting | bytes 524288
Async XLA Ops:
  0.7 1.6 %copy-start = (f32[2,4,256,256]{3,2,1,0:T(8,128)S(1)}, f32[2,4,256,256]{3,2,1,0:T(8,128)}, u32[]{:S(2)}) copy-start(f32[2,4,256,256]{3,2,1,0:T(8,128)} %probe_hbm.1) | copy-start | bytes 6291460
  2.2 1.1 %copy-start.1 = (f32[3,256,256]{2,1,0:T(8,128)S(1)}, f32[3,256,256]{2,1,0:T(8,128)}, u32[]{:S(2)}) copy-start(f32[3,256,256]{2,1,0:T(8,128)} %meas_hbm.1) | copy-start | bytes 2359300
  3.4 1.0 %copy-start.2 = (f32[2,128,512]{2,1,0:T(8,128)S(1)}, f32[2,128,512]{2,1,0:T(8,128)}, u32[]{:S(2)}) copy-start(f32[2,128,512]{2,1,0:T(8,128)} %obj_hbm.1) | copy-start | bytes 1572868
  4.4 1.0 %copy-start.3 = (bf16[512,512]{1,0:T(8,128)(2,1)S(1)}, bf16[512,512]{1,0:T(8,128)(2,1)}, u32[]{:S(2)}) copy-start(bf16[512,512]{1,0:T(8,128)(2,1)} %constant.5.clone.turned_hbm) | copy-start | bytes 1572868
  5.5 1.0 %copy-start.4 = (bf16[512,512]{1,0:T(8,128)(2,1)S(1)}, bf16[512,512]{1,0:T(8,128)(2,1)}, u32[]{:S(2)}) copy-start(bf16[512,512]{1,0:T(8,128)(2,1)} %constant.4.clone.plain_hbm) | copy-start | bytes 1572868
  6.5 0.7 %copy-start.5 = (s32[3]{0:T(128)S(1)}, s32[3]{0:T(128)}, u32[]{:S(2)}) copy-start(s32[3]{0:T(128)} %row_hbm.1) | copy-start | bytes 40
  7.2 0.7 %copy-start.6 = (s32[3]{0:T(128)S(1)}, s32[3]{0:T(128)}, u32[]{:S(2)}) copy-start(s32[3]{0:T(128)} %col_hbm.1) | copy-start | bytes 40

commit v3 on v2

--- a/solution.py
+++ b/solution.py
@@ -3,7 +3,6 @@
 
 import jax
 import jax.numpy as jnp
-import numpy as np
 from jax import lax
 from jax.experimental import pallas as pl
 from jax.experimental.pallas import tpu as pltpu
@@ -12,20 +11,32 @@
 MESH = pl.DeviceIdType.MESH
 
 
+def sine_of(step, period):
+    step = jnp.bitwise_and(step, period - 1)
+    step = jnp.where(step >= period // 2, step - period, step)
+    step = jnp.where(step > period // 4, period // 2 - step, step)
+    step = jnp.where(step < -(period // 4), -(period // 2) - step, step)
+    x = step.astype(jnp.float32) * (2.0 * math.pi / period)
+    y = x * x
+    total = jnp.full_like(x, -1.0 / math.factorial(11))
+    for order in (9, 7, 5, 3, 1):
+        total = total * y + (-1.0) ** (order // 2) / math.factorial(order)
+    return x * total
+
+
 def dft_tables(pattern):
-    counter = np.arange(pattern)
-    angles = (counter[:, None] * counter[None, :] % pattern) * (2.0 * math.pi / pattern)
+    rows = lax.broadcasted_iota(jnp.int32, (pattern, pattern), 0)
+    columns = lax.broadcasted_iota(jnp.int32, (pattern, pattern), 1)
+    phases = rows * columns
     factor = 1.0 / math.sqrt(pattern)
-    real = (np.cos(angles) * factor).astype(np.float32)
-    imag = (-np.sin(angles) * factor).astype(np.float32)
-    plain = np.block([[real, -imag], [imag, real]]).astype(jnp.bfloat16)
-    turned = np.block([[real, imag], [-imag, real]]).astype(jnp.bfloat16)
-    return plain, turned
+    real = sine_of(phases + pattern // 4, pattern) * factor
+    imag = -sine_of(phases, pattern) * factor
+    return real.astype(jnp.bfloat16), imag.astype(jnp.bfloat16), (-imag).astype(jnp.bfloat16)
 
 
 def kernel(
     n, nm, chunks,
-    row_hbm, col_hbm, count_hbm, obj_hbm, probe_hbm, meas_hbm, plain_hbm, turned_hbm,
+    row_hbm, col_hbm, count_hbm, obj_hbm, probe_hbm, meas_hbm,
     out_ref,
     row_ref, col_ref, count_ref, probe_ref, meas_ref, plain_ref, turned_ref, load_s,
     ext, acc, illum, exit_ref, wave_ref, power, power_in, pp, pp_in, red_in,
@@ -68,7 +79,7 @@
     own = ext.at[:, tile : 2 * tile, :]
     pairs = (
         (probe_hbm, probe_ref), (row_hbm, row_ref), (col_hbm, col_ref), (count_hbm, count_ref),
-        (obj_hbm, own), (plain_hbm, plain_ref), (turned_hbm, turned_ref), (meas_hbm, meas_ref),
+        (obj_hbm, own), (meas_hbm, meas_ref),
     )
     loads = [pltpu.make_async_copy(a, b, load_s.at[i]) for i, (a, b) in enumerate(pairs)]
     barrier = pltpu.get_barrier_semaphore()
@@ -123,6 +134,12 @@
     for j in range(nm - 1):
         pp_copy(j).start()
 
+    real, imag, flip = dft_tables(pat)
+    for table, (high, low) in ((plain_ref, (flip, imag)), (turned_ref, (imag, flip))):
+        table[:pat, :pat] = real
+        table[pat:, pat:] = real
+        table[:pat, pat:] = high
+        table[pat:, :pat] = low
     for load in loads[1:]:
         load.wait()
     acc[...] = jnp.zeros_like(acc)
@@ -389,10 +406,9 @@
     modes = probe.shape[1]
     share = tile // nm
     chunks = min(4, share // 8)
-    plain, turned = dft_tables(pat)
     f32, bf16 = jnp.float32, jnp.bfloat16
     vmem = pl.BlockSpec(memory_space=pltpu.VMEM)
-    anywhere = pl.BlockSpec(memory_space=pl.ANY)
+    anywhere = pl.BlockSpec(memory_space=pltpu.HBM)
     dma = pltpu.SemaphoreType.DMA
     others = nm - 1
     scratch = [
@@ -403,7 +419,7 @@
         pltpu.VMEM((slots, pat, pat), f32),
         pltpu.VMEM((2 * pat, 2 * pat), bf16),
         pltpu.VMEM((2 * pat, 2 * pat), bf16),
-        dma((8,)),
+        dma((6,)),
         pltpu.VMEM((2, 3 * tile, cols), f32),
         pltpu.VMEM((2, 3 * tile, cols), f32),
         pltpu.VMEM((3 * tile, cols), f32),
@@ -431,15 +447,14 @@
     return pl.pallas_call(
         functools.partial(kernel, n, nm, chunks),
         out_shape=jax.ShapeDtypeStruct((2, share, cols), f32),
-        in_specs=[anywhere] * 8,
+        in_specs=[anywhere] * 6,
         out_specs=vmem,
         scratch_shapes=scratch,
         compiler_params=pltpu.CompilerParams(
-            collective_id=0, has_side_effects=True, vmem_limit_bytes=48 * 1024 * 1024
+            collective_id=0, has_side_effects=True, vmem_limit_bytes=64 * 1024 * 1024
         ),
     )(
-        row_offsets, col_offsets, tile_counts, object_field, probe, measured,
-        jnp.asarray(plain), jnp.asarray(turned),
+        row_offsets, col_offsets, tile_counts, object_field, probe, measured
     )
 
 

time: 47.7 us -> 42.2 us (0.88)
  local copies, waits for them, and re-layouts: 7.85 us -> 1.67 us
  Pallas kernels: 38.4 us -> 39.3 us
    unnamed x15 -> x1, local copies, waits for them, and re-layouts: 7.85 us -> 1.67 us
    pallas_call x1, Pallas kernels: 38.4 us -> 39.3 us  [local(): pl.pallas_call(functools.partial(kernel, n, nm, chunks), out_shape=jax.Sh...]
where the time goes in v3:
time: 42.2 us; the launch traced here: 41.6 us
  Pallas kernels  39.3 us (93%)
  local copies, waits for them, and re-layouts  1.67 us (4%)
  between operations  0.66 us (2%)
    pallas_call x1, Pallas kernels, local(): pl.pallas_call(functools.partial(kernel, n, nm, chunks), out_shape=jax.Sh...  39.3 us
    unnamed x1, local copies, waits for them, and re-layouts  1.67 us

profile of v3, /device:TPU:0, one launch (start us, length us, event | category | flops | bytes accessed | tf_op | source)
XLA Modules:
  0.0 41.6 jit_solution(6263164904665481628)
XLA Ops:
  0.7 39.3 %shard_map.64 = f32[2,64,512]{2,1,0:T(8,128)} custom-call(s32[3]{0:T(128)} %row_hbm.1, s32[3]{0:T(128)} %col_hbm.1, s32[1]{0:T(128)S(6)} %copy.8.count_hbm, f32[2,128,512]{2,1,0:T(8,128)} %obj_hbm.1, f32[2,4,256,256]{3,2,1,0:T(8,128)} %probe_hbm.1, f32[3,256,256]{2,1,0:T(8,128)} %meas_hbm.1), custom_call_target="tpu_custom_call" | custom-call | tf_op jit(solution)/shard_map/pallas_call | solution.py:447
  40.0 1.7 %copy.9 = f32[2,64,512]{2,1,0:T(8,128)} copy(f32[2,64,512]{2,1,0:T(8,128)} %shard_map.64) | data formatting | bytes 524288

commit v4 on v3

--- a/solution.py
+++ b/solution.py
@@ -31,7 +31,7 @@
     factor = 1.0 / math.sqrt(pattern)
     real = sine_of(phases + pattern // 4, pattern) * factor
     imag = -sine_of(phases, pattern) * factor
-    return real.astype(jnp.bfloat16), imag.astype(jnp.bfloat16), (-imag).astype(jnp.bfloat16)
+    return real, imag
 
 
 def kernel(
@@ -39,7 +39,7 @@
     row_hbm, col_hbm, count_hbm, obj_hbm, probe_hbm, meas_hbm,
     out_ref,
     row_ref, col_ref, count_ref, probe_ref, meas_ref, plain_ref, turned_ref, load_s,
-    ext, acc, illum, exit_ref, wave_ref, power, power_in, pp, pp_in, red_in,
+    base, left, right, spun, early, stage, ext, acc, illum, exit_ref, wave_ref, power, power_in, pp, pp_in, red_in,
     far_out, far_in, near_out, near_in, il_far_in, il_near_out, il_near_in,
     halo_s, halo_r, fwd_s, fwd_r, brn_s, brn_r, brf_s, brf_r,
     pow_s, pow_r, pp_s, pp_r, ilf_s, ilf_r, iln_s, iln_r,
@@ -50,7 +50,8 @@
     modes = probe_ref.shape[1]
     share = tile // nm
     piece = share // chunks
-    lift = tile - pat // 2
+    assert pat == 2 * tile
+    f32, bf16 = jnp.float32, jnp.bfloat16
 
     p = lax.axis_index("pos")
     m = lax.axis_index("mode")
@@ -82,6 +83,14 @@
         (obj_hbm, own), (meas_hbm, meas_ref),
     )
     loads = [pltpu.make_async_copy(a, b, load_s.at[i]) for i, (a, b) in enumerate(pairs)]
+    def fill(table, real, imag, sign):
+        high, wide = table.shape[0] // 2, table.shape[1] // 2
+        real = real.astype(jnp.bfloat16)
+        table[:high, :wide] = real
+        table[high:, wide:] = real
+        table[:high, wide:] = (sign * imag).astype(jnp.bfloat16)
+        table[high:, :wide] = (-sign * imag).astype(jnp.bfloat16)
+
     barrier = pltpu.get_barrier_semaphore()
     pl.semaphore_signal(barrier, inc=1, device_id=(near_dev, m), device_id_type=MESH)
     for other in others:
@@ -134,12 +143,11 @@
     for j in range(nm - 1):
         pp_copy(j).start()
 
-    real, imag, flip = dft_tables(pat)
-    for table, (high, low) in ((plain_ref, (flip, imag)), (turned_ref, (imag, flip))):
-        table[:pat, :pat] = real
-        table[pat:, pat:] = real
-        table[:pat, pat:] = high
-        table[pat:, :pat] = low
+    real, imag = dft_tables(pat)
+    base[0] = real
+    base[1] = imag
+    for table, sign in ((plain_ref, -1.0), (turned_ref, 1.0)):
+        fill(table, real, imag, sign)
     for load in loads[1:]:
         load.wait()
     acc[...] = jnp.zeros_like(acc)
@@ -151,7 +159,48 @@
             (2, tile, cols), jnp.float32
         )
 
-    for c in range(chunks):
+    line = lax.broadcasted_iota(jnp.int32, (tile, cols), 0)
+
+    def narrowed(rows, slot):
+        return pltpu.roll(rows, lax.rem(cols - col_ref[slot], cols), 1)[:, :pat]
+
+    def add_placed(total, values, slot):
+        wide = jnp.concatenate([values, jnp.zeros((pat, cols - pat), f32)], axis=1)
+        wide = pltpu.roll(wide, col_ref[slot], 1)
+        outer, below = wide[:tile], line < row_ref[slot]
+        total[:tile, :] += jnp.where(below, 0.0, outer)
+        total[tile : 2 * tile, :] += wide[tile:]
+        total[2 * tile :, :] += jnp.where(below, outer, 0.0)
+
+    def exits(s, k, part, win_re, win_im):
+        rows = slice(part * tile, (part + 1) * tile)
+        probe_re, probe_im = spun[s, 0, k, rows, :], spun[s, 1, k, rows, :]
+        exit_re = (probe_re * win_re - probe_im * win_im).astype(bf16)
+        exit_im = (probe_re * win_im + probe_im * win_re).astype(bf16)
+        stacked = jnp.concatenate([exit_re, exit_im], axis=0)
+        exit_ref[s, k, part] = stacked
+        return jnp.dot(left[s, part], stacked, preferred_element_type=f32)
+
+    def prepare(s):
+        shift = row_ref[s]
+        real, imag = (pltpu.roll(base[i], shift, 1) for i in (0, 1))
+        for part in (0, 1):
+            columns = slice(part * tile, (part + 1) * tile)
+            fill(left.at[s, part], real[:, columns], imag[:, columns], -1.0)
+        fill(right.at[s], pltpu.roll(base[0], shift, 0), pltpu.roll(base[1], shift, 0), 1.0)
+        for i in (0, 1):
+            for k in range(modes):
+                spun[s, i, k] = pltpu.roll(probe_ref[i, k], shift, 0)
+        win_re = narrowed(ext[0, tile : 2 * tile, :], s)
+        win_im = narrowed(ext[1, tile : 2 * tile, :], s)
+        for k in range(modes):
+            early[s, k] = exits(s, k, 1, win_re, win_im)
+
+    for c in range(max(chunks, slots)):
+        if c < slots:
+            prepare(c)
+        if c >= chunks:
+            continue
         halo(c).wait_recv()
 
         @pl.when(has_back)
@@ -166,64 +215,26 @@
 
     live = count_ref[0]
 
-    steps = []
-    while sum(steps) < (3 * tile - pat) // 8 - 1:
-        steps.insert(0, max(1, 2 * sum(steps[:1])))
-
-    def placed(values, slot):
-        top = lift + row_ref[slot]
-        by = lax.rem(top, 8)
-        groups = lax.div(top, 8)
-        turned_rows = pltpu.roll(values.reshape(pat // 8, 8, pat), by, 1)
-        blank = jnp.zeros((1, 8, pat), jnp.float32)
-        upper = jnp.concatenate([turned_rows, blank], axis=0)
-        lower = jnp.concatenate([blank, turned_rows], axis=0)
-        line = lax.broadcasted_iota(jnp.int32, (1, 8, pat), 1)
-        values = jnp.where(line >= by, upper, lower).reshape(pat + 8, pat)
-        wide = jnp.concatenate([values, jnp.zeros((pat + 8, cols - pat), jnp.float32)], axis=1)
-        wide = pltpu.roll(wide, col_ref[slot], 1).reshape(pat // 8 + 1, 8, cols)
-        for step in reversed(steps):
-            blank = jnp.zeros((step, 8, cols), jnp.float32)
-            far = lax.rem(lax.div(groups, step), 2) == 1
-            wide = jnp.where(
-                far,
-                jnp.concatenate([blank, wide], axis=0),
-                jnp.concatenate([wide, blank], axis=0),
-            )
-        return wide.reshape(3 * tile, cols)
-
-    def window(part, slot):
-        top = lift + row_ref[slot]
-        by = lax.rem(top, 8)
-        groups = lax.div(top, 8)
-        rows = ext[part].reshape(3 * tile // 8, 8, cols)
-        for step in steps:
-            far = lax.rem(lax.div(groups, step), 2) == 1
-            rows = jnp.where(far, rows[step:], rows[:-step])
-        turn = lax.rem(cols - col_ref[slot], cols)
-        rows = pltpu.roll(rows.reshape(pat + 8, cols), turn, 1)
-        rows = rows[:, :pat].reshape(pat // 8 + 1, 8, pat)
-        rows = pltpu.roll(rows, lax.rem(8 - by, 8), 1)
-        line = lax.broadcasted_iota(jnp.int32, (1, 8, pat), 1)
-        return jnp.where(line < 8 - by, rows[:-1], rows[1:]).reshape(pat, pat)
-
     def add_illum(s, carry):
         whole = pp[...]
         for j in range(nm - 1):
             whole = whole + pp_in[j]
         whole = jnp.where(s < live, whole, 0.0)
-        illum[...] += placed(whole, s)
+        add_placed(illum, pltpu.roll(whole, row_ref[s], 0), s)
         return carry
 
-    lax.fori_loop(0, slots, add_illum, 0)
-
-    @pl.when(has_far)
-    def _():
-        for c in range(chunks):
+    def relay(c):
+        @pl.when(has_far)
+        def _():
             forward_near(c).wait_recv()
             for j in range(nm - 1):
                 spread(far_blk, c, j, brf_s, brf_r).start()
 
+    for c in range(chunks - 1):
+        relay(c)
+    lax.fori_loop(0, slots, add_illum, 0)
+    relay(chunks - 1)
+
     def illum_far():
         return remote(
             illum.at[rows_of(far_blk, m), :], il_far_in, ilf_s.at[0], ilf_r.at[0], far_dev, m
@@ -252,20 +263,19 @@
         )
 
     def forward(s, carry):
-        win_re = window(0, s)
-        win_im = window(1, s)
-        model = jnp.zeros((pat, pat), jnp.float32)
+        below = line < row_ref[s]
+        win_re, win_im = (
+            narrowed(jnp.where(below, ext[i, 2 * tile :, :], ext[i, :tile, :]), s) for i in (0, 1)
+        )
         for k in range(modes):
-            probe_re, probe_im = probe_ref[0, k], probe_ref[1, k]
-            exit_re = (probe_re * win_re - probe_im * win_im).astype(jnp.bfloat16)
-            exit_im = (probe_re * win_im + probe_im * win_re).astype(jnp.bfloat16)
-            stacked = jnp.concatenate([exit_re, exit_im], axis=0)
-            exit_ref[s, k] = stacked
-            half = jnp.dot(plain_ref[...], stacked, preferred_element_type=jnp.float32)
-            half = half.astype(jnp.bfloat16)
-            half = jnp.concatenate([half[:pat], half[pat:]], axis=1)
-            wave = jnp.dot(half, turned_ref[...], preferred_element_type=jnp.float32)
-            wave_ref[s, k] = wave
+            half = early[s, k] + exits(s, k, 0, win_re, win_im)
+            half = half.astype(bf16)
+            stage[k * pat : (k + 1) * pat, :pat] = half[:pat]
+            stage[k * pat : (k + 1) * pat, pat:] = half[pat:]
+        wave_ref[s] = jnp.dot(stage[...], turned_ref[...], preferred_element_type=f32)
+        model = jnp.zeros((pat, pat), f32)
+        for k in range(modes):
+            wave = wave_ref[s, k * pat : (k + 1) * pat, :]
             model = model + wave[:, :pat] * wave[:, :pat] + wave[:, pat:] * wave[:, pat:]
         power[s] = model
         for j in range(nm - 1):
@@ -294,21 +304,26 @@
         numer_re = jnp.zeros((pat, pat), jnp.float32)
         numer_im = jnp.zeros((pat, pat), jnp.float32)
         for k in range(modes):
-            fixed_re = (scaling * wave_ref[s, k, :, :pat]).astype(jnp.bfloat16)
-            fixed_im = (scaling * wave_ref[s, k, :, pat:]).astype(jnp.bfloat16)
+            block = slice(k * pat, (k + 1) * pat)
+            fixed_re = (scaling * wave_ref[s, block, :pat]).astype(bf16)
+            fixed_im = (scaling * wave_ref[s, block, pat:]).astype(bf16)
             fixed = jnp.concatenate([fixed_re, fixed_im], axis=0)
-            back = jnp.dot(turned_ref[...], fixed, preferred_element_type=jnp.float32)
-            back = back.astype(jnp.bfloat16)
-            back = jnp.concatenate([back[:pat], back[pat:]], axis=1)
-            delta = jnp.dot(back, plain_ref[...], preferred_element_type=jnp.float32)
-            delta_re = delta[:, :pat] - exit_ref[s, k, :pat, :].astype(jnp.float32)
-            delta_im = delta[:, pat:] - exit_ref[s, k, pat:, :].astype(jnp.float32)
-            probe_re, probe_im = probe_ref[0, k], probe_ref[1, k]
+            back = jnp.dot(right[s], fixed, preferred_element_type=f32).astype(bf16)
+            stage[block, :pat] = back[:pat]
+            stage[block, pat:] = back[pat:]
+        wave_ref[s] = jnp.dot(stage[...], plain_ref[...], preferred_element_type=f32)
+        for k in range(modes):
+            delta = wave_ref[s, k * pat : (k + 1) * pat, :]
+            exit_re = jnp.concatenate([exit_ref[s, k, i, :tile, :] for i in (0, 1)], axis=0)
+            exit_im = jnp.concatenate([exit_ref[s, k, i, tile:, :] for i in (0, 1)], axis=0)
+            delta_re = delta[:, :pat] - exit_re.astype(f32)
+            delta_im = delta[:, pat:] - exit_im.astype(f32)
+            probe_re, probe_im = spun[s, 0, k], spun[s, 1, k]
             numer_re = numer_re + probe_re * delta_re + probe_im * delta_im
             numer_im = numer_im + probe_re * delta_im - probe_im * delta_re
         on = s < live
-        acc[0] += placed(jnp.where(on, numer_re, 0.0), s)
-        acc[1] += placed(jnp.where(on, numer_im, 0.0), s)
+        add_placed(acc.at[0], jnp.where(on, numer_re, 0.0), s)
+        add_placed(acc.at[1], jnp.where(on, numer_im, 0.0), s)
         return carry
 
     lax.fori_loop(0, slots, backward, 0)
@@ -420,11 +435,17 @@
         pltpu.VMEM((2 * pat, 2 * pat), bf16),
         pltpu.VMEM((2 * pat, 2 * pat), bf16),
         dma((6,)),
+        pltpu.VMEM((2, pat, pat), f32),
+        pltpu.VMEM((slots, 2, 2 * pat, pat), bf16),
+        pltpu.VMEM((slots, 2 * pat, 2 * pat), bf16),
+        pltpu.VMEM((slots, 2, modes, pat, pat), f32),
+        pltpu.VMEM((slots, modes, 2 * pat, pat), f32),
+        pltpu.VMEM((modes * pat, 2 * pat), bf16),
         pltpu.VMEM((2, 3 * tile, cols), f32),
         pltpu.VMEM((2, 3 * tile, cols), f32),
         pltpu.VMEM((3 * tile, cols), f32),
-        pltpu.VMEM((slots, modes, 2 * pat, pat), bf16),
-        pltpu.VMEM((slots, modes, pat, 2 * pat), f32),
+        pltpu.VMEM((slots, modes, 2, pat, pat), bf16),
+        pltpu.VMEM((slots, modes * pat, 2 * pat), f32),
         pltpu.VMEM((slots, pat, pat), f32),
         pltpu.VMEM((slots, others, pat, pat), f32),
         pltpu.VMEM((pat, pat), f32),

time: 42.2 us -> 40.8 us (0.967)
  Pallas kernels: 39.3 us -> 38.3 us
    pallas_call x1, Pallas kernels: 39.3 us -> 38.3 us  [local(): pl.pallas_call(functools.partial(kernel, n, nm, chunks), out_shape=jax.Sh...]
where the time goes in v4:
time: 40.8 us; the launch traced here: 40.6 us
  Pallas kernels  38.3 us (94%)
  local copies, waits for them, and re-layouts  1.67 us (4%)
  between operations  0.66 us (2%)
    pallas_call x1, Pallas kernels, local(): pl.pallas_call(functools.partial(kernel, n, nm, chunks), out_shape=jax.Sh...  38.3 us
    unnamed x1, local copies, waits for them, and re-layouts  1.67 us

profile of v4, /device:TPU:0, one launch (start us, length us, event | category | flops | bytes accessed | tf_op | source)
XLA Modules:
  0.0 40.6 jit_solution(10815483162200702748)
XLA Ops:
  0.7 38.3 %shard_map.64 = f32[2,64,512]{2,1,0:T(8,128)} custom-call(s32[3]{0:T(128)} %row_hbm.1, s32[3]{0:T(128)} %col_hbm.1, s32[1]{0:T(128)S(6)} %copy.8.count_hbm, f32[2,128,512]{2,1,0:T(8,128)} %obj_hbm.1, f32[2,4,256,256]{3,2,1,0:T(8,128)} %probe_hbm.1, f32[3,256,256]{2,1,0:T(8,128)} %meas_hbm.1), custom_call_target="tpu_custom_call" | custom-call | tf_op jit(solution)/shard_map/pallas_call | solution.py:468
  39.0 1.7 %copy.9 = f32[2,64,512]{2,1,0:T(8,128)} copy(f32[2,64,512]{2,1,0:T(8,128)} %shard_map.64) | data formatting | bytes 524288

commit v5 on v4

--- a/solution.py
+++ b/solution.py
@@ -39,7 +39,7 @@
     row_hbm, col_hbm, count_hbm, obj_hbm, probe_hbm, meas_hbm,
     out_ref,
     row_ref, col_ref, count_ref, probe_ref, meas_ref, plain_ref, turned_ref, load_s,
-    base, left, right, spun, early, stage, ext, acc, illum, exit_ref, wave_ref, power, power_in, pp, pp_in, red_in,
+    base, left, right, fixed_ref, spun, early, stage, delta_ref, ext, acc, illum, exit_ref, wave_ref, power, power_in, pp, pp_in, red_in,
     far_out, far_in, near_out, near_in, il_far_in, il_near_out, il_near_in,
     halo_s, halo_r, fwd_s, fwd_r, brn_s, brn_r, brf_s, brf_r,
     pow_s, pow_r, pp_s, pp_r, ilf_s, ilf_r, iln_s, iln_r,
@@ -164,13 +164,17 @@
     def narrowed(rows, slot):
         return pltpu.roll(rows, lax.rem(cols - col_ref[slot], cols), 1)[:, :pat]
 
-    def add_placed(total, values, slot):
-        wide = jnp.concatenate([values, jnp.zeros((pat, cols - pat), f32)], axis=1)
-        wide = pltpu.roll(wide, col_ref[slot], 1)
-        outer, below = wide[:tile], line < row_ref[slot]
-        total[:tile, :] += jnp.where(below, 0.0, outer)
-        total[tile : 2 * tile, :] += wide[tile:]
-        total[2 * tile :, :] += jnp.where(below, outer, 0.0)
+    def widened(values, slot):
+        blank = jnp.zeros((tile, cols - pat), f32)
+        return pltpu.roll(jnp.concatenate([values, blank], axis=1), col_ref[slot], 1)
+
+    def add_outer(total, values, slot):
+        wide, below = widened(values, slot), line < row_ref[slot]
+        total[:tile, :] += jnp.where(below, 0.0, wide)
+        total[2 * tile :, :] += jnp.where(below, wide, 0.0)
+
+    def add_inner(total, values, slot):
+        total[tile : 2 * tile, :] += widened(values, slot)
 
     def exits(s, k, part, win_re, win_im):
         rows = slice(part * tile, (part + 1) * tile)
@@ -187,7 +191,10 @@
         for part in (0, 1):
             columns = slice(part * tile, (part + 1) * tile)
             fill(left.at[s, part], real[:, columns], imag[:, columns], -1.0)
-        fill(right.at[s], pltpu.roll(base[0], shift, 0), pltpu.roll(base[1], shift, 0), 1.0)
+        real, imag = (pltpu.roll(base[i], shift, 0) for i in (0, 1))
+        for part in (0, 1):
+            rows = slice(part * tile, (part + 1) * tile)
+            fill(right.at[s, part], real[rows], imag[rows], 1.0)
         for i in (0, 1):
             for k in range(modes):
                 spun[s, i, k] = pltpu.roll(probe_ref[i, k], shift, 0)
@@ -220,7 +227,9 @@
         for j in range(nm - 1):
             whole = whole + pp_in[j]
         whole = jnp.where(s < live, whole, 0.0)
-        add_placed(illum, pltpu.roll(whole, row_ref[s], 0), s)
+        whole = pltpu.roll(whole, row_ref[s], 0)
+        add_outer(illum, whole[:tile], s)
+        add_inner(illum, whole[tile:], s)
         return carry
 
     def relay(c):
@@ -295,38 +304,48 @@
 
     illum_near().start()
 
-    def backward(s, carry):
+    def numerators(s, part):
+        for k in range(modes):
+            back = jnp.dot(right[s, part], fixed_ref[s, k], preferred_element_type=f32)
+            back = back.astype(bf16)
+            stage[k * tile : (k + 1) * tile, :pat] = back[:tile]
+            stage[k * tile : (k + 1) * tile, pat:] = back[tile:]
+        delta_ref[...] = jnp.dot(
+            stage[: modes * tile, :], plain_ref[...], preferred_element_type=f32
+        )
+        numer_re = jnp.zeros((tile, pat), f32)
+        numer_im = jnp.zeros((tile, pat), f32)
+        rows = slice(part * tile, (part + 1) * tile)
+        for k in range(modes):
+            delta = delta_ref[k * tile : (k + 1) * tile, :]
+            delta_re = delta[:, :pat] - exit_ref[s, k, part, :tile, :].astype(f32)
+            delta_im = delta[:, pat:] - exit_ref[s, k, part, tile:, :].astype(f32)
+            probe_re, probe_im = spun[s, 0, k, rows, :], spun[s, 1, k, rows, :]
+            numer_re = numer_re + probe_re * delta_re + probe_im * delta_im
+            numer_im = numer_im + probe_re * delta_im - probe_im * delta_re
+        on = s < live
+        return jnp.where(on, numer_re, 0.0), jnp.where(on, numer_im, 0.0)
+
+    def backward_outer(s, carry):
         model = power[s]
         for j in range(nm - 1):
             power_copy(s, j).wait_recv()
             model = model + power_in[s, j]
         scaling = jnp.sqrt(meas_ref[s]) / jnp.maximum(jnp.sqrt(model), 1.0)
-        numer_re = jnp.zeros((pat, pat), jnp.float32)
-        numer_im = jnp.zeros((pat, pat), jnp.float32)
         for k in range(modes):
             block = slice(k * pat, (k + 1) * pat)
-            fixed_re = (scaling * wave_ref[s, block, :pat]).astype(bf16)
-            fixed_im = (scaling * wave_ref[s, block, pat:]).astype(bf16)
-            fixed = jnp.concatenate([fixed_re, fixed_im], axis=0)
-            back = jnp.dot(right[s], fixed, preferred_element_type=f32).astype(bf16)
-            stage[block, :pat] = back[:pat]
-            stage[block, pat:] = back[pat:]
-        wave_ref[s] = jnp.dot(stage[...], plain_ref[...], preferred_element_type=f32)
-        for k in range(modes):
-            delta = wave_ref[s, k * pat : (k + 1) * pat, :]
-            exit_re = jnp.concatenate([exit_ref[s, k, i, :tile, :] for i in (0, 1)], axis=0)
-            exit_im = jnp.concatenate([exit_ref[s, k, i, tile:, :] for i in (0, 1)], axis=0)
-            delta_re = delta[:, :pat] - exit_re.astype(f32)
-            delta_im = delta[:, pat:] - exit_im.astype(f32)
-            probe_re, probe_im = spun[s, 0, k], spun[s, 1, k]
-            numer_re = numer_re + probe_re * delta_re + probe_im * delta_im
-            numer_im = numer_im + probe_re * delta_im - probe_im * delta_re
-        on = s < live
-        add_placed(acc.at[0], jnp.where(on, numer_re, 0.0), s)
-        add_placed(acc.at[1], jnp.where(on, numer_im, 0.0), s)
+            fixed_ref[s, k, :pat, :] = (scaling * wave_ref[s, block, :pat]).astype(bf16)
+            fixed_ref[s, k, pat:, :] = (scaling * wave_ref[s, block, pat:]).astype(bf16)
+        for i, numer in enumerate(numerators(s, 0)):
+            add_outer(acc.at[i], numer, s)
         return carry
 
-    lax.fori_loop(0, slots, backward, 0)
+    def backward_inner(s, carry):
+        for i, numer in enumerate(numerators(s, 1)):
+            add_inner(acc.at[i], numer, s)
+        return carry
+
+    lax.fori_loop(0, slots, backward_outer, 0)
 
     blocks = (far_blk, near_blk, 1)
 
@@ -336,7 +355,7 @@
             red_s.at[j, b], red_r.at[j, b], p, others[j],
         )
 
-    for b in range(3):
+    for b in (0, 1):
         for j in range(nm - 1):
             reduce_copy(b, j).start()
 
@@ -359,6 +378,9 @@
             near_out.at[:, part, :], near_in.at[:, part, :], rn_s.at[c], rn_r.at[c], near_dev, m
         )
 
+    first = slots // 3
+    second = slots - slots // 3
+    lax.fori_loop(0, first, backward_inner, 0)
     far_out[...] = reduced(0)
 
     @pl.when(has_far)
@@ -367,8 +389,8 @@
             far_copy(c).start()
 
     near_out[...] = reduced(1)
-    for c in range(chunks):
-
+
+    def pass_on(c):
         @pl.when(has_back)
         def _():
             part = pl.ds(c * piece, piece)
@@ -376,6 +398,14 @@
             near_out[:, part, :] = near_out[:, part, :] + far_in[:, part, :]
 
         near_copy(c).start()
+
+    lax.fori_loop(first, second, backward_inner, 0)
+    pass_on(0)
+    lax.fori_loop(second, slots, backward_inner, 0)
+    for j in range(nm - 1):
+        reduce_copy(2, j).start()
+    for c in range(1, chunks):
+        pass_on(c)
 
     own_sum = reduced(2)
     illum_near().wait_recv()
@@ -437,10 +467,12 @@
         dma((6,)),
         pltpu.VMEM((2, pat, pat), f32),
         pltpu.VMEM((slots, 2, 2 * pat, pat), bf16),
-        pltpu.VMEM((slots, 2 * pat, 2 * pat), bf16),
+        pltpu.VMEM((slots, 2, pat, 2 * pat), bf16),
+        pltpu.VMEM((slots, modes, 2 * pat, pat), bf16),
         pltpu.VMEM((slots, 2, modes, pat, pat), f32),
         pltpu.VMEM((slots, modes, 2 * pat, pat), f32),
         pltpu.VMEM((modes * pat, 2 * pat), bf16),
+        pltpu.VMEM((modes * tile, 2 * pat), f32),
         pltpu.VMEM((2, 3 * tile, cols), f32),
         pltpu.VMEM((2, 3 * tile, cols), f32),
         pltpu.VMEM((3 * tile, cols), f32),

time: 40.8 us -> 38.6 us (0.946)
  Pallas kernels: 38.3 us -> 36.1 us
    pallas_call x1, Pallas kernels: 38.3 us -> 36.1 us  [local(): pl.pallas_call(functools.partial(kernel, n, nm, chunks), out_shape=jax.Sh...]
where the time goes in v5:
time: 38.6 us; the launch traced here: 38.4 us
  Pallas kernels  36.1 us (94%)
  local copies, waits for them, and re-layouts  1.67 us (4%)
  between operations  0.66 us (2%)
    pallas_call x1, Pallas kernels, local(): pl.pallas_call(functools.partial(kernel, n, nm, chunks), out_shape=jax.Sh...  36.1 us
    unnamed x1, local copies, waits for them, and re-layouts  1.67 us

profile of v5, /device:TPU:0, one launch (start us, length us, event | category | flops | bytes accessed | tf_op | source)
XLA Modules:
  0.0 38.4 jit_solution(5982530752622589716)
XLA Ops:
  0.7 36.1 %shard_map.64 = f32[2,64,512]{2,1,0:T(8,128)} custom-call(s32[3]{0:T(128)} %row_hbm.1, s32[3]{0:T(128)} %col_hbm.1, s32[1]{0:T(128)S(6)} %copy.8.count_hbm, f32[2,128,512]{2,1,0:T(8,128)} %obj_hbm.1, f32[2,4,256,256]{3,2,1,0:T(8,128)} %probe_hbm.1, f32[3,256,256]{2,1,0:T(8,128)} %meas_hbm.1), custom_call_target="tpu_custom_call" | custom-call | tf_op jit(solution)/shard_map/pallas_call | solution.py:500
  36.8 1.7 %copy.9 = f32[2,64,512]{2,1,0:T(8,128)} copy(f32[2,64,512]{2,1,0:T(8,128)} %shard_map.64) | data formatting | bytes 524288

commit v6 on v5

--- a/solution.py
+++ b/solution.py
@@ -107,6 +107,11 @@
     greeted = has_far.astype(jnp.int32) + has_back.astype(jnp.int32)
     for load in loads:
         load.start()
+    real, imag = dft_tables(pat)
+    base[0] = real
+    base[1] = imag
+    for table, sign in ((plain_ref, -1.0), (turned_ref, 1.0)):
+        fill(table, real, imag, sign)
     pl.semaphore_wait(barrier, nm + greeted)
 
     def halo(c):
@@ -143,11 +148,6 @@
     for j in range(nm - 1):
         pp_copy(j).start()
 
-    real, imag = dft_tables(pat)
-    base[0] = real
-    base[1] = imag
-    for table, sign in ((plain_ref, -1.0), (turned_ref, 1.0)):
-        fill(table, real, imag, sign)
     for load in loads[1:]:
         load.wait()
     acc[...] = jnp.zeros_like(acc)
@@ -185,7 +185,7 @@
         exit_ref[s, k, part] = stacked
         return jnp.dot(left[s, part], stacked, preferred_element_type=f32)
 
-    def prepare(s):
+    def turn_tables(s):
         shift = row_ref[s]
         real, imag = (pltpu.roll(base[i], shift, 1) for i in (0, 1))
         for part in (0, 1):
@@ -195,17 +195,27 @@
         for part in (0, 1):
             rows = slice(part * tile, (part + 1) * tile)
             fill(right.at[s, part], real[rows], imag[rows], 1.0)
+
+    def turn_probes(s):
         for i in (0, 1):
             for k in range(modes):
-                spun[s, i, k] = pltpu.roll(probe_ref[i, k], shift, 0)
+                spun[s, i, k] = pltpu.roll(probe_ref[i, k], row_ref[s], 0)
+
+    def start_products(s):
         win_re = narrowed(ext[0, tile : 2 * tile, :], s)
         win_im = narrowed(ext[1, tile : 2 * tile, :], s)
         for k in range(modes):
             early[s, k] = exits(s, k, 1, win_re, win_im)
 
-    for c in range(max(chunks, slots)):
-        if c < slots:
-            prepare(c)
+    work = [
+        functools.partial(do, s)
+        for s in range(slots)
+        for do in (turn_tables, turn_probes, start_products)
+    ]
+
+    for c in range(max(chunks, len(work))):
+        if c < len(work):
+            work[c]()
         if c >= chunks:
             continue
         halo(c).wait_recv()
@@ -450,7 +460,7 @@
     slots, pat = measured.shape[:2]
     modes = probe.shape[1]
     share = tile // nm
-    chunks = min(4, share // 8)
+    chunks = min(8, share // 8)
     f32, bf16 = jnp.float32, jnp.bfloat16
     vmem = pl.BlockSpec(memory_space=pltpu.VMEM)
     anywhere = pl.BlockSpec(memory_space=pltpu.HBM)

time: 38.6 us -> 38.3 us (level)
  no operation moved by 1% of the time
where the time goes in v6:
time: 38.3 us; the launch traced here: 38.2 us
  Pallas kernels  35.9 us (94%)
  local copies, waits for them, and re-layouts  1.67 us (4%)
  between operations  0.66 us (2%)
    pallas_call x1, Pallas kernels, local(): pl.pallas_call(functools.partial(kernel, n, nm, chunks), out_shape=jax.Sh...  35.9 us
    unnamed x1, local copies, waits for them, and re-layouts  1.67 us

profile of v6, /device:TPU:0, one launch (start us, length us, event | category | flops | bytes accessed | tf_op | source)
XLA Modules:
  0.0 38.2 jit_solution(15652749199382411136)
XLA Ops:
  0.7 35.9 %shard_map.64 = f32[2,64,512]{2,1,0:T(8,128)} custom-call(s32[3]{0:T(128)} %row_hbm.1, s32[3]{0:T(128)} %col_hbm.1, s32[1]{0:T(128)S(6)} %copy.8.count_hbm, f32[2,128,512]{2,1,0:T(8,128)} %obj_hbm.1, f32[2,4,256,256]{3,2,1,0:T(8,128)} %probe_hbm.1, f32[3,256,256]{2,1,0:T(8,128)} %meas_hbm.1), custom_call_target="tpu_custom_call" | custom-call | tf_op jit(solution)/shard_map/pallas_call | solution.py:510
  36.5 1.7 %copy.9 = f32[2,64,512]{2,1,0:T(8,128)} copy(f32[2,64,512]{2,1,0:T(8,128)} %shard_map.64) | data formatting | bytes 524288

commit v7 on v6

--- a/solution.py
+++ b/solution.py
@@ -249,10 +249,9 @@
             for j in range(nm - 1):
                 spread(far_blk, c, j, brf_s, brf_r).start()
 
-    for c in range(chunks - 1):
+    for c in range(chunks):
         relay(c)
     lax.fori_loop(0, slots, add_illum, 0)
-    relay(chunks - 1)
 
     def illum_far():
         return remote(
@@ -509,12 +508,12 @@
     ]
     return pl.pallas_call(
         functools.partial(kernel, n, nm, chunks),
-        out_shape=jax.ShapeDtypeStruct((2, share, cols), f32),
+        out_shape=pltpu.VMEM((2, share, cols), f32),
         in_specs=[anywhere] * 6,
         out_specs=vmem,
         scratch_shapes=scratch,
         compiler_params=pltpu.CompilerParams(
-            collective_id=0, has_side_effects=True, vmem_limit_bytes=64 * 1024 * 1024
+            collective_id=0, has_side_effects=True, vmem_limit_bytes=65200 * 1024
         ),
     )(
         row_offsets, col_offsets, tile_counts, object_field, probe, measured

time: 38.3 us -> 37.3 us (0.974)
  local copies, waits for them, and re-layouts: 1.67 us -> 0.71 us
    unnamed x1, local copies, waits for them, and re-layouts: 1.67 us -> 0.71 us
where the time goes in v7:
time: 37.3 us; the launch traced here: 37.1 us
  Pallas kernels  35.8 us (96%)
  local copies, waits for them, and re-layouts  0.71 us (2%)
  between operations  0.66 us (2%)
    pallas_call x1, Pallas kernels, local(): pl.pallas_call(functools.partial(kernel, n, nm, chunks), out_shape=pltpu....  35.8 us

profile of v7, /device:TPU:0, one launch (start us, length us, event | category | flops | bytes accessed | tf_op | source)
XLA Modules:
  0.0 37.1 jit_solution(3232535024453717676)
XLA Ops:
  0.7 35.8 %shard_map.64 = f32[2,64,512]{2,1,0:T(8,128)S(1)} custom-call(s32[3]{0:T(128)} %row_hbm.1, s32[3]{0:T(128)} %col_hbm.1, s32[1]{0:T(128)S(6)} %copy.9.count_hbm, f32[2,128,512]{2,1,0:T(8,128)} %obj_hbm.1, f32[2,4,256,256]{3,2,1,0:T(8,128)} %probe_hbm.1, f32[3,256,256]{2,1,0:T(8,128)} %meas_hbm.1), custom_call_target="tpu_custom_call" | custom-call | tf_op jit(solution)/shard_map/pallas_call | solution.py:509
  36.4 0.7 %copy.8 = f32[2,64,512]{2,1,0:T(8,128)} copy(f32[2,64,512]{2,1,0:T(8,128)S(1)} %shard_map.64) | data formatting | bytes 524288

commit v8 on v7

--- a/solution.py
+++ b/solution.py
@@ -112,35 +112,36 @@
     base[1] = imag
     for table, sign in ((plain_ref, -1.0), (turned_ref, 1.0)):
         fill(table, real, imag, sign)
-    pl.semaphore_wait(barrier, nm + greeted)
-
-    def halo(c):
-        return remote(
-            obj_hbm.at[:, rows_of(0, m, c, piece), :], ext.at[:, rows_of(far_blk, m, c, piece), :],
-            halo_s.at[c], halo_r.at[c], near_dev, m,
-        )
-
-    def forward_near(c):
-        return remote(
-            ext.at[:, rows_of(near_blk, m, c, piece), :],
-            ext.at[:, rows_of(far_blk, m, c, piece), :],
-            fwd_s.at[c], fwd_r.at[c], back_dev, m,
-        )
-
-    def spread(block, c, j, s, r):
-        where = rows_of(block, m, c, piece)
-        return remote(
-            ext.at[:, where, :], ext.at[:, where, :], s.at[j, c], r.at[j, c], p, others[j]
-        )
-
-    for c in range(chunks):
-        halo(c).start()
-
     loads[0].wait()
     total = jnp.zeros((pat, pat), jnp.float32)
     for k in range(modes):
         total = total + probe_ref[0, k] * probe_ref[0, k] + probe_ref[1, k] * probe_ref[1, k]
     pp[...] = total
+    for load in loads[1:]:
+        load.wait()
+    pl.semaphore_wait(barrier, nm + greeted)
+
+    def halo(c):
+        return remote(
+            obj_hbm.at[:, rows_of(0, m, c, piece), :], ext.at[:, rows_of(far_blk, m, c, piece), :],
+            halo_s.at[c], halo_r.at[c], near_dev, m,
+        )
+
+    def forward_near(c):
+        return remote(
+            ext.at[:, rows_of(near_blk, m, c, piece), :],
+            ext.at[:, rows_of(far_blk, m, c, piece), :],
+            fwd_s.at[c], fwd_r.at[c], back_dev, m,
+        )
+
+    def spread(block, c, j, s, r):
+        where = rows_of(block, m, c, piece)
+        return remote(
+            ext.at[:, where, :], ext.at[:, where, :], s.at[j, c], r.at[j, c], p, others[j]
+        )
+
+    for c in range(chunks):
+        halo(c).start()
 
     def pp_copy(j):
         return remote(pp, pp_in.at[j], pp_s.at[j], pp_r.at[j], p, others[j])
@@ -148,8 +149,6 @@
     for j in range(nm - 1):
         pp_copy(j).start()
 
-    for load in loads[1:]:
-        load.wait()
     acc[...] = jnp.zeros_like(acc)
     illum[...] = jnp.zeros_like(illum)
 

time: 37.3 us -> 37.8 us (1.013)
  Pallas kernels: 35.8 us -> 36.2 us
    pallas_call x1, Pallas kernels: 35.8 us -> 36.2 us  [local(): pl.pallas_call(functools.partial(kernel, n, nm, chunks), out_shape=pltpu....]
where the time goes in v8:
time: 37.8 us; the launch traced here: 37.6 us
  Pallas kernels  36.2 us (96%)
  local copies, waits for them, and re-layouts  0.71 us (2%)
  between operations  0.66 us (2%)
    pallas_call x1, Pallas kernels, local(): pl.pallas_call(functools.partial(kernel, n, nm, chunks), out_shape=pltpu....  36.2 us

profile of v8, /device:TPU:0, one launch (start us, length us, event | category | flops | bytes accessed | tf_op | source)
XLA Modules:
  0.0 37.6 jit_solution(17352316357590434928)
XLA Ops:
  0.7 36.2 %shard_map.64 = f32[2,64,512]{2,1,0:T(8,128)S(1)} custom-call(s32[3]{0:T(128)} %row_hbm.1, s32[3]{0:T(128)} %col_hbm.1, s32[1]{0:T(128)S(6)} %copy.9.count_hbm, f32[2,128,512]{2,1,0:T(8,128)} %obj_hbm.1, f32[2,4,256,256]{3,2,1,0:T(8,128)} %probe_hbm.1, f32[3,256,256]{2,1,0:T(8,128)} %meas_hbm.1), custom_call_target="tpu_custom_call" | custom-call | tf_op jit(solution)/shard_map/pallas_call | solution.py:508
  36.9 0.7 %copy.8 = f32[2,64,512]{2,1,0:T(8,128)} copy(f32[2,64,512]{2,1,0:T(8,128)S(1)} %shard_map.64) | data formatting | bytes 524288
